TPU v7x, 32 devices: a whole 2x2x4 slice. The times are simulated.
32 devices in a mesh: clip: 16 (over z, x, core), slab: 2 (over y).
Axes of the slice: x: 2, y: 2, z: 4, core: 2. Of those that a mesh axis runs over, the one named last changes fastest.
Arguments:
- inputs: bfloat16 [128, 64, 8, 512], P('clip', 'slab'), may hold values from -6 to 6
- grad_mask: int32 [128, 64, 8], P('clip', 'slab'), may hold values from 0 to 1, as said below
- cotangent: bfloat16 [128, 64, 8, 512], P('clip', 'slab'), may hold values from -6 to 6
- ln1_gain: bfloat16 [512], P(('clip', 'slab')), may hold values from 0.099609375 to 1.8984375
- ln1_bias: bfloat16 [512], P(('clip', 'slab')), may hold values from -3 to 3
- w_qkv: bfloat16 [512, 1536], P(('clip', 'slab')), may hold values from -0.25 to 0.25
- q_bias: bfloat16 [512], P(('clip', 'slab')), may hold values from -3 to 3
- v_bias: bfloat16 [512], P(('clip', 'slab')), may hold values from -3 to 3
- w_proj: bfloat16 [512, 512], P(('clip', 'slab')), may hold values from -1 to 1
- proj_bias: bfloat16 [512], P(('clip', 'slab')), may hold values from -3 to 3
- ln2_gain: bfloat16 [512], P(('clip', 'slab')), may hold values from 0.099609375 to 1.8984375
- ln2_bias: bfloat16 [512], P(('clip', 'slab')), may hold values from -3 to 3
- w_fc1: bfloat16 [512, 2048], P(('clip', 'slab')), may hold values from -0.25 to 0.25
- fc1_bias: bfloat16 [2048], P(('clip', 'slab')), may hold values from -3 to 3
- w_fc2: bfloat16 [2048, 512], P(('clip', 'slab')), may hold values from -0.125 to 0.125
- fc2_bias: bfloat16 [512], P(('clip', 'slab')), may hold values from -3 to 3
- pos_table: float32 [49, 16], replicated, may hold values from -4 to 4
Outputs:
- output: bfloat16 [128, 64, 8, 512], P('clip', 'slab')
- input_grad: bfloat16 [128, 64, 8, 512], P('clip', 'slab')
- ln1_gain_grad: float32 [512], P(('clip', 'slab'))
- ln1_bias_grad: float32 [512], P(('clip', 'slab'))
- w_qkv_grad: float32 [512, 1536], P(('clip', 'slab'))
- q_bias_grad: float32 [512], P(('clip', 'slab'))
- v_bias_grad: float32 [512], P(('clip', 'slab'))
- w_proj_grad: float32 [512, 512], P(('clip', 'slab'))
- proj_bias_grad: float32 [512], P(('clip', 'slab'))
- ln2_gain_grad: float32 [512], P(('clip', 'slab'))
- ln2_bias_grad: float32 [512], P(('clip', 'slab'))
- w_fc1_grad: float32 [512, 2048], P(('clip', 'slab'))
- fc1_bias_grad: float32 [2048], P(('clip', 'slab'))
- w_fc2_grad: float32 [2048, 512], P(('clip', 'slab'))
- fc2_bias_grad: float32 [512], P(('clip', 'slab'))
- pos_table_grad: float32 [49, 16], replicated
Inputs may be any that keep to these rules, and one draw needn't show every extreme that they name: grad_mask[c, t, f] is 1 where patch (t, f) of clip c receives a gradient; each clip's patches are 1 independently with a chance of that clip's own between 0.70 and 0.90.
All inputs are finite; a program needn't handle non-finite values.
Results may differ from a plain program's by a relative error of at most 0.011.
Values may be sent and summed in bfloat16 or wider, within the bound.
A program may use at most 256 MiB of HBM per device.

v0:
```python
import math

import jax
import jax.numpy as jnp
from jax import lax
from jax.sharding import PartitionSpec as P

HEADS = 16
HEAD_DIM = 32
WIN = 4
SHIFT = 2
TABLE = 49


epsilon = 1e-06
highest = lax.Precision.HIGHEST


def from_behind(block, axis, distance):
    devices = range(lax.axis_size(axis))
    route = [((i - distance) % len(devices), i) for i in devices]
    return lax.ppermute(block, axis, route)


def normalize(values, gain_row, bias_row):
    average = jnp.mean(values, -1, keepdims=True)
    centred = values - average
    variance = jnp.mean(centred * centred, -1, keepdims=True)
    return centred * lax.rsqrt(variance + epsilon) * gain_row + bias_row


def exact_gelu(values):
    return jax.nn.gelu(values, approximate=False)


def table_onehot():
    positions = jnp.arange(WIN * WIN)
    row_of = positions // WIN
    column_of = positions % WIN
    table_index = (
        (row_of[:, None] - row_of[None, :] + WIN - 1) * (2 * WIN - 1)
        + column_of[:, None]
        - column_of[None, :]
        + WIN
        - 1
    )
    return (table_index.reshape(-1)[:, None] == jnp.arange(TABLE)[None, :]).astype(jnp.float32)


def to_windows(field_grid):
    clip_count, row_count, column_count, feature_width = field_grid.shape
    blocks = field_grid.reshape(
        clip_count, row_count // WIN, WIN, column_count // WIN, WIN, feature_width
    )
    return blocks.transpose(0, 1, 3, 2, 4, 5).reshape(-1, WIN * WIN, feature_width)


def from_windows(windows, clip_count, row_count, column_count):
    feature_width = windows.shape[-1]
    blocks = windows.reshape(
        clip_count, row_count // WIN, column_count // WIN, WIN, WIN, feature_width
    )
    return blocks.transpose(0, 1, 3, 2, 4, 5).reshape(
        clip_count, row_count, column_count, feature_width
    )


def times_transposed(left, right):
    return lax.dot_general(
        left, right, (((1,), (1,)), ((), ())), preferred_element_type=jnp.float32
    )


def outer_sum(left, right):
    return lax.dot_general(
        left, right, (((0,), (0,)), ((), ())), preferred_element_type=jnp.float32
    )


def per_device(
    inputs,
    grad_mask,
    cotangent,
    ln1_gain,
    ln1_bias,
    w_qkv,
    q_bias,
    v_bias,
    w_proj,
    proj_bias,
    ln2_gain,
    ln2_bias,
    w_fc1,
    fc1_bias,
    w_fc2,
    fc2_bias,
    pos_table,
):
    (
        gain_one,
        bias_one,
        qkv_full,
        qbias_full,
        vbias_full,
        proj_full,
        pbias_full,
        gain_two,
        bias_two,
        fc1_full,
        fc1b_full,
        fc2_full,
        fc2b_full,
    ) = (
        lax.all_gather(ln1_gain, ("clip", "slab"), axis=0, tiled=True),
        lax.all_gather(ln1_bias, ("clip", "slab"), axis=0, tiled=True),
        lax.all_gather(w_qkv, ("clip", "slab"), axis=0, tiled=True),
        lax.all_gather(q_bias, ("clip", "slab"), axis=0, tiled=True),
        lax.all_gather(v_bias, ("clip", "slab"), axis=0, tiled=True),
        lax.all_gather(w_proj, ("clip", "slab"), axis=0, tiled=True),
        lax.all_gather(proj_bias, ("clip", "slab"), axis=0, tiled=True),
        lax.all_gather(ln2_gain, ("clip", "slab"), axis=0, tiled=True),
        lax.all_gather(ln2_bias, ("clip", "slab"), axis=0, tiled=True),
        lax.all_gather(w_fc1, ("clip", "slab"), axis=0, tiled=True),
        lax.all_gather(fc1_bias, ("clip", "slab"), axis=0, tiled=True),
        lax.all_gather(w_fc2, ("clip", "slab"), axis=0, tiled=True),
        lax.all_gather(fc2_bias, ("clip", "slab"), axis=0, tiled=True),
    )
    clip_count, row_count, column_count, feature_width = inputs.shape
    score_scale = 1.0 / math.sqrt(HEAD_DIM)
    float_type = jnp.float32
    half_type = jnp.bfloat16
    ahead = from_behind(inputs[:, :SHIFT], "slab", -1)
    window_rows = jnp.concatenate([inputs[:, SHIFT:], ahead], axis=1).astype(float_type)
    normed, first_pull = jax.vjp(
        normalize, window_rows, gain_one.astype(float_type), bias_one.astype(float_type)
    )
    windows = to_windows(jnp.roll(normed.astype(half_type), -SHIFT, axis=2))
    window_count = windows.shape[0]
    token_count = window_count * WIN * WIN
    head_shape = (window_count, WIN * WIN, HEADS, HEAD_DIM)
    flat_windows = windows.reshape(token_count, feature_width)
    projected = jnp.dot(flat_windows, qkv_full, preferred_element_type=float_type)
    query_heads = (
        (projected[:, :feature_width] + qbias_full.astype(float_type))
        .astype(half_type)
        .reshape(head_shape)
    )
    key_heads = (
        projected[:, feature_width : 2 * feature_width].astype(half_type).reshape(head_shape)
    )
    value_heads = (
        (projected[:, 2 * feature_width :] + vbias_full.astype(float_type))
        .astype(half_type)
        .reshape(head_shape)
    )
    onehot = table_onehot()
    position_bias = (
        jnp.dot(onehot, pos_table, precision=highest)
        .reshape(WIN * WIN, WIN * WIN, HEADS)
        .transpose(2, 0, 1)
    )
    scores = (
        jnp.einsum("wqhc,wkhc->whqk", query_heads, key_heads, preferred_element_type=float_type)
        * score_scale
        + position_bias[None]
    )
    attention = jax.nn.softmax(scores, axis=-1)
    attention_low = attention.astype(half_type)
    context = jnp.einsum(
        "whqk,wkhc->wqhc", attention_low, value_heads, preferred_element_type=float_type
    )
    context = context.astype(half_type).reshape(window_count, WIN * WIN, feature_width)
    context_grid = jnp.roll(
        from_windows(context, clip_count, row_count, column_count), SHIFT, axis=2
    )
    returned = from_behind(context_grid[:, row_count - SHIFT :], "slab", 1)
    own_flat = jnp.concatenate([returned, context_grid[:, : row_count - SHIFT]], axis=1).reshape(
        -1, feature_width
    )
    input_flat = inputs.reshape(-1, feature_width).astype(float_type)
    middle = (
        input_flat
        + jnp.dot(own_flat, proj_full, preferred_element_type=float_type)
        + pbias_full.astype(float_type)
    )
    second, second_pull = jax.vjp(
        normalize, middle, gain_two.astype(float_type), bias_two.astype(float_type)
    )
    second_low = second.astype(half_type)
    pre_act = jnp.dot(second_low, fc1_full, preferred_element_type=float_type) + fc1b_full.astype(
        float_type
    )
    hidden, gelu_pull = jax.vjp(exact_gelu, pre_act)
    hidden_low = hidden.astype(half_type)
    output = (
        middle
        + jnp.dot(hidden_low, fc2_full, preferred_element_type=float_type)
        + fc2b_full.astype(float_type)
    )
    incoming = (cotangent.astype(float_type) * grad_mask.astype(float_type)[..., None]).reshape(
        -1, feature_width
    )
    incoming_low = incoming.astype(half_type)
    fc2_grad = outer_sum(hidden_low, incoming_low)
    fc2b_grad = jnp.sum(incoming, axis=0)
    hidden_grad = times_transposed(incoming_low, fc2_full)
    pre_grad = gelu_pull(hidden_grad)[0].astype(half_type)
    fc1_grad = outer_sum(second_low, pre_grad)
    fc1b_grad = jnp.sum(pre_grad.astype(float_type), axis=0)
    second_grad = times_transposed(pre_grad, fc1_full)
    middle_part, gain_two_grad, bias_two_grad = second_pull(second_grad)
    middle_grad = incoming + middle_part
    branch_low = middle_grad.astype(half_type)
    proj_grad = outer_sum(own_flat, branch_low)
    pbias_grad = jnp.sum(branch_low.astype(float_type), axis=0)
    context_grad = (
        times_transposed(branch_low, proj_full)
        .astype(half_type)
        .reshape(clip_count, row_count, column_count, feature_width)
    )
    sent_back = from_behind(context_grad[:, :SHIFT], "slab", -1)
    window_context_grad = jnp.concatenate([context_grad[:, SHIFT:], sent_back], axis=1)
    context_heads = to_windows(jnp.roll(window_context_grad, -SHIFT, axis=2)).reshape(head_shape)
    value_grad = jnp.einsum(
        "whqk,wqhc->wkhc", attention_low, context_heads, preferred_element_type=float_type
    ).astype(half_type)
    attention_grad = jnp.einsum(
        "wqhc,wkhc->whqk", context_heads, value_heads, preferred_element_type=float_type
    )
    score_grad = (
        attention * (attention_grad - jnp.sum(attention_grad * attention, -1, keepdims=True))
    ).astype(half_type)
    bias_cells = (
        jnp.sum(score_grad.astype(float_type), axis=0)
        .transpose(1, 2, 0)
        .reshape(WIN * WIN * WIN * WIN, HEADS)
    )
    table_grad = lax.dot_general(onehot, bias_cells, (((0,), (0,)), ((), ())), precision=highest)
    query_grad = (
        jnp.einsum("whqk,wkhc->wqhc", score_grad, key_heads, preferred_element_type=float_type)
        * score_scale
    ).astype(half_type)
    key_grad = (
        jnp.einsum("whqk,wqhc->wkhc", score_grad, query_heads, preferred_element_type=float_type)
        * score_scale
    ).astype(half_type)
    query_flat = query_grad.reshape(token_count, feature_width)
    value_flat = value_grad.reshape(token_count, feature_width)
    qkv_grad_low = jnp.concatenate(
        [query_flat, key_grad.reshape(token_count, feature_width), value_flat], axis=1
    )
    qkv_grad = outer_sum(flat_windows, qkv_grad_low)
    qbias_grad = jnp.sum(query_flat.astype(float_type), axis=0)
    vbias_grad = jnp.sum(value_flat.astype(float_type), axis=0)
    normed_grad = times_transposed(qkv_grad_low, qkv_full).reshape(
        window_count, WIN * WIN, feature_width
    )
    normed_grid_grad = jnp.roll(
        from_windows(normed_grad, clip_count, row_count, column_count), SHIFT, axis=2
    )
    rows_part, gain_one_grad, bias_one_grad = first_pull(normed_grid_grad)
    halo_back = from_behind(
        rows_part[:, row_count - SHIFT :].astype(jnp.bfloat16), "slab", 1
    ).astype(jnp.float32)
    input_grad = middle_grad.reshape(
        clip_count, row_count, column_count, feature_width
    ) + jnp.concatenate([halo_back, rows_part[:, : row_count - SHIFT]], axis=1)
    shares = (
        lax.psum_scatter(gain_one_grad, ("clip", "slab"), scatter_dimension=0, tiled=True),
        lax.psum_scatter(bias_one_grad, ("clip", "slab"), scatter_dimension=0, tiled=True),
        lax.psum_scatter(qkv_grad, ("clip", "slab"), scatter_dimension=0, tiled=True),
        lax.psum_scatter(qbias_grad, ("clip", "slab"), scatter_dimension=0, tiled=True),
        lax.psum_scatter(vbias_grad, ("clip", "slab"), scatter_dimension=0, tiled=True),
        lax.psum_scatter(proj_grad, ("clip", "slab"), scatter_dimension=0, tiled=True),
        lax.psum_scatter(pbias_grad, ("clip", "slab"), scatter_dimension=0, tiled=True),
        lax.psum_scatter(gain_two_grad, ("clip", "slab"), scatter_dimension=0, tiled=True),
        lax.psum_scatter(bias_two_grad, ("clip", "slab"), scatter_dimension=0, tiled=True),
        lax.psum_scatter(fc1_grad, ("clip", "slab"), scatter_dimension=0, tiled=True),
        lax.psum_scatter(fc1b_grad, ("clip", "slab"), scatter_dimension=0, tiled=True),
        lax.psum_scatter(fc2_grad, ("clip", "slab"), scatter_dimension=0, tiled=True),
        lax.psum_scatter(fc2b_grad, ("clip", "slab"), scatter_dimension=0, tiled=True),
    )
    table_total = lax.psum(table_grad, ("clip", "slab"))
    output = output.reshape(clip_count, row_count, column_count, feature_width).astype(half_type)
    return (
        output,
        input_grad.astype(half_type),
        shares[0],
        shares[1],
        shares[2],
        shares[3],
        shares[4],
        shares[5],
        shares[6],
        shares[7],
        shares[8],
        shares[9],
        shares[10],
        shares[11],
        shares[12],
        table_total,
    )


def solution(mesh):
    in_specs = (
        P("clip", "slab", None, None),
        P("clip", "slab", None),
        P("clip", "slab", None, None),
        P(("clip", "slab")),
        P(("clip", "slab")),
        P(("clip", "slab"), None),
        P(("clip", "slab")),
        P(("clip", "slab")),
        P(("clip", "slab"), None),
        P(("clip", "slab")),
        P(("clip", "slab")),
        P(("clip", "slab")),
        P(("clip", "slab"), None),
        P(("clip", "slab")),
        P(("clip", "slab"), None),
        P(("clip", "slab")),
        P(),
    )
    out_specs = (
        P("clip", "slab", None, None),
        P("clip", "slab", None, None),
        P(("clip", "slab")),
        P(("clip", "slab")),
        P(("clip", "slab"), None),
        P(("clip", "slab")),
        P(("clip", "slab")),
        P(("clip", "slab"), None),
        P(("clip", "slab")),
        P(("clip", "slab")),
        P(("clip", "slab")),
        P(("clip", "slab"), None),
        P(("clip", "slab")),
        P(("clip", "slab"), None),
        P(("clip", "slab")),
        P(),
    )
    return jax.shard_map(
        per_device, mesh=mesh, in_specs=in_specs, out_specs=out_specs, check_vma=False
    )
```

profile of v0, /device:TPU:0, one launch (start us, length us, event | category | flops | bytes accessed | tf_op | source)
XLA Modules:
  0.0 911.9 jit_solution(11847113344048075693)
XLA Ops:
  9.8 3.0 collective-permute-start
  16.9 40.3 %all-reduce.19 = (bf16[512]{0:T(512)(128)(2,1)S(1)}, bf16[512]{0:T(512)(128)(2,1)S(1)}, bf16[512]{0:T(512)(128)(2,1)S(1)}, bf16[512]{0:T(512)(128)(2,1)S(1)}, bf...) all-reduce(bf16[512]{0:T(512)(128)(2,1)S(1)} %dynamic-update-slice., ...), channel_id=1, replica_groups=mesh['clip'=16,'slab'=2] {'clip','slab'}, use_global_device_ids=true, to_apply=%add.1 | all-reduce | flops 6144 | bytes 24576
  57.5 2.7 fusion.50
  71.7 2.6 copy.171
  76.4 5.5 fusion.68
  82.1 3.4 fusion.43
  85.5 10.3 %reshape.244 = bf16[128,16,16,32]{3,2,1,0:T(8,128)(2,1)} reshape(bf16[2048,512]{1,0:T(8,128)(2,1)} %get-tuple-element.48) | data formatting | bytes 4194304 | tf_op jit(solution)/shard_map/reshape | solution.py:146
  95.8 7.1 reshape.245
  102.8 10.4 %reshape.243 = bf16[128,16,16,32]{3,2,1,0:T(8,128)(2,1)} reshape(bf16[2048,512]{1,0:T(8,128)(2,1)} %get-tuple-element.49) | data formatting | bytes 4194304 | tf_op jit(solution)/shard_map/reshape | solution.py:154
  113.3 13.6 %fusion.18 = f32[128,16,16,16]{2,3,1,0:T(8,128)} fusion(bf16[128,16,16,32]{3,2,1,0:T(8,128)(2,1)} %reshape.245, bf16[128,16,16,32]{3,2,1,0:T(8,128)(2,1)} %reshape.244), kind=kOutput, calls=%fused_computation.42 | convolution fusion | flops 33554432 | bytes 6291456 | tf_op jit(solution)/shard_map/wqhc,wkhc->whqk/dot_general | solution.py:163
  126.8 25.2 %fusion.66 = (f32[128,16,16]{2,1,0:T(8,128)S(1)}, f32[128,16,16,16]{2,3,1,0:T(8,128)}) fusion(f32[128,16,16,16]{2,3,1,0:T(8,128)} %fusion.18, f32[16,16,16]{1,2,0:T(8,128)S(1)} %bitcast.82), kind=kOutput, calls=%fused_computation.131 | output fusion | flops 3145743 | bytes 4341760 | tf_op jit(solution)/shard_map/sub | solution.py:167
  152.0 14.0 %convert_bitcast_fusion.1 = bf16[128,16,16,32]{3,1,2,0:T(8,128)(2,1)} fusion(bf16[128,16,16,32]{3,2,1,0:T(8,128)(2,1)} %reshape.243, f32[128,16,16,16]{2,3,1,0:T(8,128)} %get-tuple-element.57, f32[128,16,16]{2,1,0:T(8,128)S(1)} %get-tuple-element.56), kind=kOutput, calls=%fused_computation.30 | convolution fusion | flops 35651584 | bytes 6422528 | tf_op jit(solution)/shard_map/whqk,wkhc->wqhc/dot_general | solution.py:169
  166.0 10.8 %copy.115 = bf16[128,16,16,32]{3,2,1,0:T(8,128)(2,1)} copy(bf16[128,16,16,32]{3,1,2,0:T(8,128)(2,1)} %convert_bitcast_fusion.1) | data formatting | bytes 4194304 | tf_op jit(solution)/shard_map/convert_element_type | solution.py:172
  176.8 10.8 %reshape_reshape.13 = bf16[8,8,2,4,4,512]{5,4,3,2,1,0:T(4,128)(2,1)S(1)} reshape(bf16[128,16,16,32]{3,2,1,0:T(8,128)(2,1)} %copy.115) | data formatting | bytes 4194304 | tf_op jit(solution)/shard_map/reshape;reshape | solution.py:60
  190.1 3.0 collective-permute-start.1
  193.1 68.3 %all_gather.44 = bf16[512,512]{1,0:T(8,128)(2,1)S(1)} all-gather(bf16[16,512]{1,0:T(8,128)(2,1)S(1)} %copy-done.38), channel_id=1, replica_groups=mesh['clip'=16,'slab'=2] {'clip','slab'}, dimensions={0}, use_global_device_ids=true | all-gather | bytes 540672 | tf_op jit(solution)/shard_map/all_gather | solution.py:119
  267.6 44.9 %multiply_convert_fusion.3 = (bf16[2048,2048]{1,0:T(8,128)(2,1)}, f32[2048,2048]{1,0:T(8,128)}, f32[2048,2048]{1,0:T(8,128)}) fusion(f32[2048]{0:T(1024)S(1)} %convert_element_type.148, bf16[512,2048]{1,0:T(8,128)(2,1)} %all-gather.6.cloned.1.call-done, f32[2048,512]{1,0:T(8,128)} %copy-done.7, f32[512]{0:T(512)S(1)} %convert_element_type.146, ...), kind=kOutput, calls=%fused_computation.12 | convolution fusion | flops 4577034240 | bytes 48263168 | tf_op jit(solution)/shard_map/dot_general | solution.py:190
  312.5 20.1 %convert_reduce_fusion.1 = (f32[2048]{0:T(1024)}, bf16[2048,2048]{1,0:T(8,128)(2,1)}) fusion(f32[2048,2048]{1,0:T(8,128)} %get-tuple-element.47, bf16[2048,512]{1,0:T(8,128)(2,1)S(1)} %copy-done.18, bf16[2048,512]{1,0:T(8,128)(2,1)} %all-gather.8.cloned.1.call-done, f32[2048,2048]{1,0:T(8,128)} %get-tuple-element.60, f32[2048]{0:T(1024)S(1)} %convert_element_type.148), kind=kOutput, calls=%fused_computation.4 | convolution fusion | flops 4366268416 | bytes 46153728 | tf_op jit(solution)/shard_map/dot_general | solution.py:69
  332.7 11.9 %multiply_reduce_fusion.1 = (f32[512]{0:T(512)}, f32[2048]{0:T(1024)S(1)}, f32[512]{0:T(512)}, f32[2048,512]{1,0:T(8,128)S(1)}) fusion(f32[2048,512]{1,0:T(8,128)} %copy-done.7, f32[2048]{0:T(1024)S(1)} %fusion.57, f32[2048]{0:T(1024)S(1)} %broadcast_multiply_fusion.1, f32[512]{0:T(512)S(1)} %convert_element_type.145, ...), kind=kOutput, calls=%fused_computation.75 | convolution fusion | flops 4303352832 | bytes 18905088 | tf_op jit(solution)/shard_map/dot_general | solution.py:69
  353.9 3.2 copy_dynamic-update-slice_fusion
  359.9 6.5 reshape_reshape.14
  366.4 14.0 %convert_reduce_fusion.2 = (f32[16,32]{1,0:T(8,128)}, bf16[128,16,16,32]{3,1,2,0:T(8,128)(2,1)}) fusion(bf16[128,16,16,32]{3,2,1,0:T(8,128)(2,1)} %reshape_reshape.14, f32[128,16,16,16]{2,3,1,0:T(8,128)} %get-tuple-element.57, f32[128,16,16]{2,1,0:T(8,128)S(1)} %copy-done.27), kind=kOutput, calls=%fused_computation.5 | convolution fusion | flops 37748224 | bytes 6424576 | tf_op jit(solution)/shard_map/whqk,wqhc->wkhc/dot_general | solution.py:224
  380.4 20.4 %multiply_reduce_fusion = (f32[128,16,16]{2,1,0:T(8,128)S(1)}, f32[128,16,16,16]{2,3,1,0:T(8,128)}) fusion(f32[128,16,16,16]{2,3,1,0:T(8,128)} %get-tuple-element.57, f32[128,16,16]{2,1,0:T(8,128)S(1)} %copy-done.27, bf16[128,16,16,32]{3,2,1,0:T(8,128)(2,1)} %reshape.243, bf16[128,16,16,32]{3,2,1,0:T(8,128)(2,1)} %reshape_reshape.14), kind=kOutput, calls=%fused_computation.10 | convolution fusion | flops 35094528 | bytes 8650752 | tf_op jit(solution)/shard_map/wqhc,wkhc->whqk/dot_general | solution.py:227
  400.8 15.7 %convert_reduce_fusion = (f32[16,16,16]{1,2,0:T(8,128)S(1)}, bf16[128,16,16,16]{2,3,1,0:T(8,128)(2,1)}) fusion(f32[128,16,16,16]{2,3,1,0:T(8,128)} %get-tuple-element.63, f32[128,16,16]{2,1,0:T(8,128)S(1)} %get-tuple-element.62, f32[128,16,16,16]{2,3,1,0:T(8,128)} %get-tuple-element.57, f32[128,16,16]{2,1,0:T(8,128)S(1)} %copy-done.27), kind=kLoop, calls=%fused_computation.3 | loop fusion | flops 3141632 | bytes 5521408 | tf_op jit(solution)/shard_map/reduce_sum | solution.py:234
  416.5 10.7 %convert_reduce_fusion.3 = (f32[16,32]{1,0:T(8,128)S(1)}, bf16[128,16,16,32]{3,1,2,0:T(8,128)(2,1)}) fusion(bf16[128,16,16,16]{2,3,1,0:T(8,128)(2,1)} %get-tuple-element.41, bf16[128,16,16,32]{3,2,1,0:T(8,128)(2,1)} %reshape.245), kind=kOutput, calls=%fused_computation.6 | convolution fusion | flops 37748224 | bytes 5244928 | tf_op jit(solution)/shard_map/whqk,wkhc->wqhc/dot_general | solution.py:240
  427.2 13.6 %fusion.29 = bf16[128,16,16,32]{3,1,2,0:T(8,128)(2,1)} fusion(bf16[128,16,16,16]{2,3,1,0:T(8,128)(2,1)} %get-tuple-element.41, bf16[128,16,16,32]{3,2,1,0:T(8,128)(2,1)} %reshape.244), kind=kOutput, calls=%fused_computation.49 | convolution fusion | flops 35651584 | bytes 5242880 | tf_op jit(solution)/shard_map/whqk,wqhc->wkhc/dot_general | solution.py:244
  440.8 10.9 %copy.130 = bf16[128,16,16,32]{3,2,1,0:T(8,128)(2,1)} copy(bf16[128,16,16,32]{3,1,2,0:T(8,128)(2,1)} %get-tuple-element.67) | data formatting | bytes 4194304 | tf_op jit(solution)/shard_map/convert_element_type | solution.py:226
  451.6 11.1 %reshape.255 = bf16[2048,512]{1,0:T(8,128)(2,1)S(1)} reshape(bf16[128,16,16,32]{3,2,1,0:T(8,128)(2,1)} %copy.130) | data formatting | bytes 4194304 | tf_op jit(solution)/shard_map/reshape | solution.py:248
  462.7 10.9 %copy.128 = bf16[128,16,16,32]{3,2,1,0:T(8,128)(2,1)} copy(bf16[128,16,16,32]{3,1,2,0:T(8,128)(2,1)} %fusion.29) | data formatting | bytes 4194304 | tf_op jit(solution)/shard_map/convert_element_type | solution.py:246
  473.6 12.0 %reshape.254 = bf16[2048,512]{1,0:T(8,128)(2,1)} reshape(bf16[128,16,16,32]{3,2,1,0:T(8,128)(2,1)} %copy.128) | data formatting | bytes 4194304 | tf_op jit(solution)/shard_map/reshape | solution.py:250
  485.6 10.9 %copy.126 = bf16[128,16,16,32]{3,2,1,0:T(8,128)(2,1)} copy(bf16[128,16,16,32]{3,1,2,0:T(8,128)(2,1)} %get-tuple-element.65) | data formatting | bytes 4194304 | tf_op jit(solution)/shard_map/convert_element_type | solution.py:242
  496.5 12.2 %reshape.253 = bf16[2048,512]{1,0:T(8,128)(2,1)} reshape(bf16[128,16,16,32]{3,2,1,0:T(8,128)(2,1)} %copy.126) | data formatting | bytes 4194304 | tf_op jit(solution)/shard_map/reshape | solution.py:247
  511.2 2.6 copy-done.28
  513.9 5.1 fusion.70
  519.1 11.6 %fusion.62 = f32[512,2048]{1,0:T(8,128)} fusion(bf16[2048,2048]{1,0:T(8,128)(2,1)} %get-tuple-element.69, f32[2048,512]{1,0:T(8,128)} %copy-done.7, f32[512]{0:T(512)S(1)} %copy-done.48, f32[512]{0:T(512)S(1)} %copy-done.44, f32[2048]{0:T(1024)S(1)} %copy-done.37, f32[2048]{0:T(1024)S(1)} %copy-done.32), kind=kOutput, calls=%fused_computation.128 | convolution fusion | flops 4300210176 | bytes 16797696 | tf_op jit(solution)/shard_map/dot_general | solution.py:75
  532.3 10.1 %fusion.71 = f32[2048,512]{1,0:T(8,128)} fusion(bf16[2048,2048]{1,0:T(8,128)(2,1)} %get-tuple-element.46, bf16[2048,512]{1,0:T(8,128)(2,1)S(1)} %copy-done.19), kind=kOutput, calls=%fused_computation.136 | convolution fusion | flops 4294967296 | bytes 14680064 | tf_op jit(solution)/shard_map/dot_general | solution.py:75
  543.1 11.5 %add_convert_fusion.1 = bf16[2048,512]{1,0:T(8,128)(2,1)} fusion(f32[2048,512]{1,0:T(8,128)} %copy-done.7, bf16[2048,2048]{1,0:T(8,128)(2,1)} %get-tuple-element.46, bf16[2048,512]{1,0:T(8,128)(2,1)} %all-gather.8.cloned.1.call-done, f32[512]{0:T(512)S(1)} %convert_element_type.150), kind=kOutput, calls=%fused_computation.79 | convolution fusion | flops 4298113024 | bytes 16779264 | tf_op jit(solution)/shard_map/dot_general | solution.py:197
  554.6 5.1 fusion.69
  559.6 5.2 reshape_reshape.15
  564.8 5.4 copy.131
  570.2 5.3 reshape.256
  575.5 3.0 slice_reduce_fusion.1
  578.6 3.0 slice_reduce_fusion
  583.7 3.2 fusion.40
  592.9 37.4 %all-reduce.18 = (f32[512]{0:T(512)S(1)}, f32[512]{0:T(512)S(1)}, f32[512]{0:T(512)S(1)}, f32[512]{0:T(512)S(1)}, f32[512]{0:T(512)S(1)}, /*index=5*/f32[512]{0:...) all-reduce(f32[512]{0:T(512)S(1)} %get-tuple-element.18, ...), channel_id=2, replica_groups=mesh['clip'=16,'slab'=2] {'clip','slab'}, use_global_device_ids=true, to_apply=%region_12.13.clone | all-reduce | flops 6928 | bytes 55424
  635.6 5.5 fusion.45
  641.1 122.1 %reduce-scatter.9.cloned.1.call-done = f32[16,2048]{1,0:T(8,128)} async-done(((f32[512,2048]{1,0:T(8,128)}), f32[16,2048]{1,0:T(8,128)}) %reduce-scatter.9.cloned.1.call-update) | async-done | bytes 131088 | tf_op jit(solution)/shard_map/reduce_scatter | solution.py:278
  763.2 141.4 %reduce-scatter.11.cloned.1.call-done = f32[64,512]{1,0:T(8,128)} async-done(((f32[2048,512]{1,0:T(8,128)}), f32[64,512]{1,0:T(8,128)}) %reduce-scatter.11.cloned.1.call-update) | async-done | bytes 131088 | tf_op jit(solution)/shard_map/reduce_scatter | solution.py:280
  (251 shorter events, 59.0 us)
Async XLA Ops:
  7.2 56.5 %copy-start = (f32[49,16]{0,1:T(8,128)S(1)}, f32[49,16]{0,1:T(8,128)}, u32[]{:S(2)}) copy-start(f32[49,16]{0,1:T(8,128)} %param.33) | copy-start | bytes 9412
  7.2 7.4 copy-start.53
  7.2 7.7 copy-start.54
  7.2 7.9 copy-start.55
  7.2 8.1 copy-start.56
  7.2 8.4 copy-start.57
  7.3 8.6 copy-start.58
  7.3 8.9 copy-start.59
  7.3 9.1 copy-start.60
  7.3 9.3 %copy-start.61 = (bf16[64]{0:T(256)(128)(2,1)S(1)}, bf16[64]{0:T(256)(128)(2,1)}, u32[]{:S(2)}) copy-start(bf16[64]{0:T(256)(128)(2,1)} %param.30) | copy-start | bytes 388
  7.3 50.1 %copy-start.35 = (s32[8,32,8]{1,2,0:T(8,128)S(1)}, s32[8,32,8]{1,2,0:T(8,128)}, u32[]{:S(2)}) copy-start(s32[8,32,8]{1,2,0:T(8,128)} %param.18) | copy-start | bytes 24580
  7.3 69.1 %all-gather.4.cloned.1.call-start = ((), (), s32[]{:S(2)}) async-start(), calls=%async_computation.4 | async-start | bytes 1622016 | tf_op jit(solution)/shard_map/all_gather | solution.py:116
  8.0 259.6 %all-gather.6.cloned.1.call-start = ((), (), s32[]{:S(2)}) async-start(), calls=%async_computation.5 | async-start | bytes 2162688 | tf_op jit(solution)/shard_map/all_gather | solution.py:123
  8.8 303.7 %all-gather.8.cloned.1.call-start = ((), (), s32[]{:S(2)}) async-start(), calls=%async_computation.6 | async-start | bytes 2162688 | tf_op jit(solution)/shard_map/all_gather | solution.py:125
  9.8 54.5 %collective-permute-start = (bf16[8,2,8,512]{3,2,1,0:T(8,128)(2,1)S(1)}, bf16[8,2,8,512]{3,2,1,0:T(8,128)(2,1)S(1)}, u32[]{:S(2)}, u32[]{:S(2)}) collective-permute-start(bf16[8,2,8,512]{3,2,1,0:T(8,128)(2,1)S(1)} %slice.66), channel_id=1, source_target_pairs={{1,0},{0,1},{3,2},{2,3},{5,4},{4,5},{7,6},{6,7},{9,8},{8,9},{11,10... | collective-permute-start | bytes 393224 | tf_op jit(solution)/shard_map/ppermute | solution.py:22
  12.8 628.3 %reduce-scatter.7.cloned.1.call-start = ((), (), s32[]{:S(2)}) async-start(), calls=%async_computation.8 | async-start | bytes 1081344 | tf_op jit(solution)/shard_map/reduce_scatter | solution.py:274
  14.6 51.6 %copy-start.2 = (bf16[8,30,8,512]{3,2,1,0:T(8,128)(2,1)}, bf16[8,30,8,512]{3,2,1,0:T(8,128)(2,1)S(1)}, u32[]{:S(2)}) copy-start(bf16[8,30,8,512]{3,2,1,0:T(8,128)(2,1)S(1)} %slice.65) | copy-start | bytes 5898244
  57.2 9.1 copy-start.33
  57.4 6.4 copy-start.49
  64.2 280.4 %copy-start.43 = (f32[512]{0:T(512)}, f32[512]{0:T(512)S(1)}, u32[]{:S(2)}) copy-start(f32[512]{0:T(512)S(1)} %convert_element_type.145) | copy-start | bytes 6148
  64.2 203.4 %copy-start.47 = (f32[512]{0:T(512)}, f32[512]{0:T(512)S(1)}, u32[]{:S(2)}) copy-start(f32[512]{0:T(512)S(1)} %convert_element_type.146) | copy-start | bytes 6148
  152.0 14.0 %copy-start.26 = (f32[128,16,16]{2,1,0:T(8,128)}, f32[128,16,16]{2,1,0:T(8,128)S(1)}, u32[]{:S(2)}) copy-start(f32[128,16,16]{2,1,0:T(8,128)S(1)} %get-tuple-element.56) | copy-start | bytes 393220
  190.1 71.3 %collective-permute-start.1 = (bf16[8,2,8,512]{3,0,2,1:T(8,128)(2,1)S(1)}, bf16[8,2,8,512]{3,0,2,1:T(8,128)(2,1)S(1)}, u32[]{:S(2)}, u32[]{:S(2)}) collective-permute-start(bf16[8,2,8,512]{3,0,2,1:T(8,128)(2,1)S(1)} %pad_maximum_fusion.5), channel_id=1, source_target_pairs={{1,0},{0,1},{3,2},{2,3},{5,4},{4,5},{7,6},{6,7},{9,8},{8,9},{11,10... | collective-permute-start | bytes 393224 | tf_op jit(solution)/shard_map/ppermute | solution.py:22
  264.7 79.9 %copy-start.31 = (f32[2048]{0:T(1024)}, f32[2048]{0:T(1024)S(1)}, u32[]{:S(2)}) copy-start(f32[2048]{0:T(1024)S(1)} %broadcast_multiply_fusion.1) | copy-start | bytes 24580
  267.5 45.0 %copy-start.29 = (f32[2048]{0:T(1024)}, f32[2048]{0:T(1024)S(1)}, u32[]{:S(2)}) copy-start(f32[2048]{0:T(1024)S(1)} %multiply_reduce_fusion.3) | copy-start | bytes 24580
  267.5 77.1 %copy-start.36 = (f32[2048]{0:T(1024)}, f32[2048]{0:T(1024)S(1)}, u32[]{:S(2)}) copy-start(f32[2048]{0:T(1024)S(1)} %fusion.57) | copy-start | bytes 24580
  267.6 45.0 %copy-start.18 = (bf16[2048,512]{1,0:T(8,128)(2,1)S(1)}, bf16[2048,512]{1,0:T(8,128)(2,1)}, u32[]{:S(2)}) copy-start(bf16[2048,512]{1,0:T(8,128)(2,1)} %bitcast_convert_fusion) | copy-start | bytes 6291460
  332.6 11.9 %copy-start.30 = (f32[2048]{0:T(1024)S(1)}, f32[2048]{0:T(1024)}, u32[]{:S(2)}) copy-start(f32[2048]{0:T(1024)} %copy-done.29) | copy-start | bytes 24580
  332.6 12.0 %copy-start.8 = (f32[2048,512]{1,0:T(8,128)S(1)}, f32[2048,512]{1,0:T(8,128)}, u32[]{:S(2)}) copy-start(f32[2048,512]{1,0:T(8,128)} %copy-done.7) | copy-start | bytes 12582916
  353.3 5.0 collective-permute-start.2
  357.1 284.0 %reduce-scatter.5.cloned.1.call-start = ((), (), s32[]{:S(2)}) async-start(), calls=%async_computation.7 | async-start | bytes 3244032 | tf_op jit(solution)/shard_map/reduce_scatter | solution.py:271
  359.9 6.6 copy-start.27
  513.9 5.2 copy-start.32
  513.9 5.2 copy-start.37
  513.9 5.2 copy-start.44
  513.9 5.2 copy-start.48
  519.0 244.2 %reduce-scatter.9.cloned.1.call-start = ((), (), s32[]{:S(2)}) async-start(), calls=%async_computation.9 | async-start | bytes 4325376 | tf_op jit(solution)/shard_map/reduce_scatter | solution.py:278
  530.7 373.9 %reduce-scatter.11.cloned.1.call-start = ((), (), s32[]{:S(2)}) async-start(), calls=%async_computation.10 | async-start | bytes 4325376 | tf_op jit(solution)/shard_map/reduce_scatter | solution.py:280
  542.4 12.1 %slice-start = ((s8[6291456]{0:T(1024)(128)(4,1)}), s8[2097152]{0:T(1024)(128)(4,1)S(1)}, s32[]{:S(2)}) async-start(s8[6291456]{0:T(1024)(128)(4,1)} %bitcast.79), calls=%async_computation.11 | async-start | bytes 4194304
  543.1 11.5 %slice-start.1 = ((s8[6291456]{0:T(1024)(128)(4,1)}), s8[4194304]{0:T(1024)(128)(4,1)S(1)}, s32[]{:S(2)}) async-start(s8[6291456]{0:T(1024)(128)(4,1)} %bitcast.79), calls=%async_computation.12 | async-start | bytes 8388608
  543.1 11.5 %copy-start.52 = (bf16[512,1536]{1,0:T(8,128)(2,1)S(1)}, bf16[512,1536]{1,0:T(8,128)(2,1)}, u32[]{:S(2)}) copy-start(bf16[512,1536]{1,0:T(8,128)(2,1)} %all-gather.4.cloned.1.call-done) | copy-start | bytes 4718596
  588.9 4.0 copy-start.39
  588.9 3.9 copy-start.40
  588.9 3.9 copy-start.42
  588.9 3.9 copy-start.45
  588.9 3.9 copy-start.46
  591.9 43.7 %collective-permute-start.3 = (bf16[8,2,8,512]{3,2,1,0:T(8,128)(2,1)S(1)}, bf16[8,2,8,512]{3,2,1,0:T(8,128)(2,1)S(1)}, u32[]{:S(2)}, u32[]{:S(2)}) collective-permute-start(bf16[8,2,8,512]{3,2,1,0:T(8,128)(2,1)S(1)} %slice.110), channel_id=1, source_target_pairs={{1,0},{0,1},{3,2},{2,3},{5,4},{4,5},{7,6},{6,7},{9,8},{8,9},{11,10... | collective-permute-start | bytes 393224 | tf_op jit(solution)/shard_map/ppermute | solution.py:22
  635.6 269.0 %copy-start.1 = (f32[49,16]{0,1:T(8,128)S(1)}, f32[49,16]{0,1:T(8,128)}, u32[]{:S(2)}) copy-start(f32[49,16]{0,1:T(8,128)} %param.33) | copy-start | bytes 9412
  (27 other events, 60.6 us)
Sparse Core Ops, SparseCore 0:
  11.0 57.8 all-gather.3
  72.0 55.5 all-gather.5
  130.7 55.3 all-gather.7
  357.2 132.0 reduce-scatter.6
  519.1 100.1 reduce-scatter.4
  622.1 141.0 reduce-scatter.8
  766.1 138.3 reduce-scatter.10
where the time goes:
time: 917 us; the launch traced here: 912 us
  waiting for transfers between devices  266 us (29%)
  matrix products  217 us (24%)
  local copies, waits for them, and re-layouts  184 us (20%)
  blocking collectives  146 us (16%)
  other arithmetic  74.7 us (8%)
  between operations  15.7 us (2%)
    reduce_scatter x1, waiting for transfers between devices, per_device(): lax.psum_scatter(fc2_grad, ('clip', 'slab'), scatter_dimension=0, tiled=T...  141 us
    reduce_scatter x1, waiting for transfers between devices, per_device(): lax.psum_scatter(fc1_grad, ('clip', 'slab'), scatter_dimension=0, tiled=T...  122 us
    unnamed x2, blocking collectives  77.7 us
    all_gather x1, blocking collectives, per_device(): lax.all_gather(w_proj, ('clip', 'slab'), axis=0, tiled=True)  68.3 us
    dot_general x1, matrix products, per_device(): jnp.dot(second_low, fc1_full, preferred_element_type=float_type)  44.9 us
    dot_general x4, matrix products, times_transposed(): lax.dot_general(left, right, (((1,), (1,)), ((), ())), preferred_element_...  38.4 us
    dot_general x4, matrix products, outer_sum(): lax.dot_general(left, right, (((0,), (0,)), ((), ())), preferred_element_...  29 us
    sub x1, other arithmetic, per_device(): attention = jax.nn.softmax(scores, axis=-1)  25.2 us
  transfers between devices with their start and end apart: 11, of which 3 were waited for; matrix products, arithmetic and copies ran while one was open for 47% of the time, Pallas kernels for 0%

commit v1 on v0

--- a/solution.py
+++ b/solution.py
@@ -1,9 +1,391 @@
+import functools
 import math
 
 import jax
 import jax.numpy as jnp
 from jax import lax
+from jax.experimental import pallas as pl
+from jax.experimental.pallas import tpu as pltpu
 from jax.sharding import PartitionSpec as P
+
+F32 = jnp.float32
+BF = jnp.bfloat16
+MESH = pl.DeviceIdType.MESH
+SCALE = 1.0 / math.sqrt(32.0)
+NT = (((1,), (1,)), ((), ()))
+TN = (((0,), (0,)), ((), ()))
+VM = pl.BlockSpec(memory_space=pltpu.VMEM)
+HB = pl.BlockSpec(memory_space=pl.ANY)
+UNROLL = 16
+
+
+def dot(a, b, dims=(((1,), (0,)), ((), ()))):
+    return lax.dot_general(a, b, dims, preferred_element_type=F32)
+
+
+def tree(xs, op=lambda a, b: a + b):
+    xs = list(xs)
+    while len(xs) > 1:
+        xs = [op(xs[i], xs[i + 1]) if i + 1 < len(xs) else xs[i] for i in range(0, len(xs), 2)]
+    return xs[0]
+
+
+def tile(ref, i):
+    return ref[pl.ds(pl.multiple_of(i * 16, 16), 16), :]
+
+
+def row(ref, i):
+    return jnp.broadcast_to(ref[pl.ds(i, 1), :], (16, 128))
+
+
+def pair_products(a_ref, a0, b_ref, b0):
+    def body(d, acc):
+        ad = tile(a_ref, a0 + d)
+        return tuple(acc[q] + ad * row(b_ref, (b0 + d) * 16 + q) for q in range(16))
+
+    return lax.fori_loop(
+        0, 32, body, tuple(jnp.zeros((16, 128), F32) for _ in range(16)), unroll=UNROLL
+    )
+
+
+def weighted(ws, b_ref, b0, o_ref, o0, scale):
+    def body(d, carry):
+        parts = []
+        for k in range(4):
+            t = ws[4 * k] * row(b_ref, (b0 + d) * 16 + 4 * k)
+            for q in range(4 * k + 1, 4 * k + 4):
+                t = t + ws[q] * row(b_ref, (b0 + d) * 16 + q)
+            parts.append(t)
+        s = (parts[0] + parts[1]) + (parts[2] + parts[3])
+        if scale is not None:
+            s = s * scale
+        o_ref[pl.ds(pl.multiple_of((o0 + d) * 16, 16), 16), :] = s.astype(BF).astype(F32)
+        return carry
+
+    lax.fori_loop(0, 32, body, 0, unroll=UNROLL)
+
+
+class Place:
+    def __init__(self):
+        self.clip = lax.axis_index("clip")
+        self.y = lax.axis_index("slab")
+        self.c = self.clip % 2
+        self.x = (self.clip // 2) % 2
+        self.z = self.clip // 4
+        self.rank8 = self.x * 4 + self.c * 2 + self.y
+        base = self.x * 2 + self.c
+        self.along_z = [(((self.z + d) % 4) * 4 + base, self.y) for d in (1, 2, 3)]
+        self.over_x = (self.clip + 2 - 4 * self.x, self.y)
+        self.over_y = (self.clip, 1 - self.y)
+        self.over_core = (self.clip + 1 - 2 * self.c, self.y)
+
+    def greet(self):
+        barrier = pltpu.get_barrier_semaphore()
+        others = self.along_z + [self.over_x, self.over_y, self.over_core]
+        for other in others:
+            pl.semaphore_signal(barrier, inc=1, device_id=other, device_id_type=MESH)
+        pl.semaphore_wait(barrier, len(others))
+
+
+def remote(src, dst, ssem, rsem, to):
+    return pltpu.make_async_remote_copy(
+        src_ref=src, dst_ref=dst, send_sem=ssem, recv_sem=rsem, device_id=to, device_id_type=MESH
+    )
+
+
+class Gather:
+    def __init__(self, place, pieces, ssem, rsem):
+        self.copies = []
+        z, x, c, y = place.z, place.x, place.c, place.y
+        for k, (buf, c0, n, first_x) in enumerate(pieces):
+            cols = pl.ds(c0, n)
+
+            def cp(ix, s, to, k=k, buf=buf, cols=cols):
+                ref = buf.at[ix + (slice(None), cols)]
+                return remote(ref, ref, ssem.at[k, s], rsem.at[k, s], to)
+
+            al = slice(None)
+            steps = [[cp((z, x, c, y), d, place.along_z[d]) for d in range(3)]]
+            if first_x:
+                steps.append([cp((al, x, c, y), 3, place.over_x)])
+                steps.append([cp((al, al, c, y), 4, place.over_y)])
+            else:
+                steps.append([cp((al, x, c, y), 3, place.over_y)])
+                steps.append([cp((al, x, c, al), 4, place.over_x)])
+            steps.append([cp((al, al, c, al), 5, place.over_core)])
+            self.copies.append(steps)
+
+    def start(self, k, s):
+        for copy in self.copies[k][s]:
+            copy.start()
+
+    def advance(self, k, s):
+        for copy in self.copies[k][s]:
+            copy.wait_recv()
+        if s < 3:
+            self.start(k, s + 1)
+
+    def close(self):
+        for steps in self.copies:
+            for step in steps:
+                for copy in step:
+                    copy.wait_send()
+
+
+def spots(p):
+    i, j = p // 4, p % 4
+    return (i * 8 + (j + 2) % 8, i * 8 + (j + 6) % 8)
+
+
+def gathered(ref, lo, hi):
+    return jnp.concatenate([ref[pl.ds(lo, 64, stride=32), :], ref[pl.ds(hi, 64, stride=32), :]], axis=0)
+
+
+def small_block(place, small_refs, fc1b_ref, scr):
+    scr[...] = jnp.zeros_like(scr)
+    for k, ref in enumerate(small_refs):
+        scr[k : k + 1, 0:16] = ref[...].astype(F32)
+    lane = lax.broadcasted_iota(jnp.int32, (128, 128), 1)
+    src = lax.broadcasted_iota(jnp.int32, (128, 128), 0)
+    sel = ((lane == place.rank8 * 16 + src) & (src < 16)).astype(F32).astype(BF)
+    vectors = dot(scr[...].astype(BF), sel)
+    scr[0:1, 0:64] = fc1b_ref[...].astype(F32)
+    half = ((lane == place.y * 64 + src) & (src < 64)).astype(F32).astype(BF)
+    wide = dot(scr[0:1, :].astype(BF), half)
+    r = lax.broadcasted_iota(jnp.int32, (16, 128), 0)
+    return jnp.where(
+        r < 8,
+        vectors,
+        jnp.where(r == 8 + place.x * 2 + place.c, jnp.broadcast_to(wide, (16, 128)), 0.0),
+    ).astype(BF)
+
+
+def k1_body(
+    x_ref, wq_ref, wp_ref, w1_ref, w2_ref, s0, s1, s2, s3, s4, s5, s6, s7, fb_ref, bt_ref,
+    ctx_ref, wqb, wpb, w1b, w2b, par_ref, qkv_save, att_save, ctxt_ref, normt_ref, nt_ref, rs_ref,
+    xs, ntf, g_ref, ct_ref, cs_ref, a_ref, qb, halo, chalo, gains, scr,
+    ssem, rsem, hss, hrs, lsem, osem,
+):
+    me = Place()
+    z, x, c, y = me.z, me.x, me.c, me.y
+    own = [
+        pltpu.make_async_copy(src, buf.at[z, x, c, y], osem.at[i])
+        for i, (src, buf) in enumerate(((wp_ref, wpb), (w1_ref, w1b), (w2_ref, w2b)))
+    ]
+    for cp in own:
+        cp.start()
+    wqb[z, x, c, y, :, 0:128] = small_block(me, (s0, s1, s2, s3, s4, s5, s6, s7), fb_ref, scr)
+    for g in range(4):
+        for k in range(3):
+            wqb[z, x, c, y, :, 128 + g * 384 + k * 128 : 256 + g * 384 + k * 128] = wq_ref[
+                :, k * 512 + g * 128 : k * 512 + g * 128 + 128
+            ]
+    pieces = [(wqb, 0, 512, True)] + [(wqb, 128 + g * 384, 384, g % 2 == 0) for g in (1, 2, 3)]
+    pieces += [(wpb, 0, 256, True), (wpb, 256, 256, False)]
+    pieces += [(w1b, 0, 1024, True), (w1b, 1024, 1024, False)]
+    pieces += [(w2b, 0, 256, True), (w2b, 256, 256, False)]
+    gat = Gather(me, pieces, ssem, rsem)
+    me.greet()
+    for k in range(4):
+        gat.start(k, 0)
+    xhalo = remote(x_ref.at[:, 0:16, :], halo, hss.at[4], hrs.at[4], me.over_y)
+    xhalo.start()
+    for b in range(8):
+        for k in range(4):
+            xs[k, b * 256 : b * 256 + 240, :] = x_ref[b, 16:256, k * 128 : k * 128 + 128].astype(F32)
+    gat.advance(0, 0)
+    gat.advance(1, 0)
+    xhalo.wait_recv()
+    for b in range(8):
+        for k in range(4):
+            xs[k, b * 256 + 240 : b * 256 + 256, :] = halo[b, :, k * 128 : k * 128 + 128].astype(F32)
+
+    def norm_block(p):
+        lo, hi = spots(p)
+        turned = jnp.concatenate([gathered(xs.at[k], lo, hi).T for k in range(4)], axis=0)
+        mean = jnp.mean(turned, 0, keepdims=True)
+        cen = turned - mean
+        rs = lax.rsqrt(jnp.mean(cen * cen, 0, keepdims=True) + 1e-6)
+        ntf[:, p * 128 : (p + 1) * 128] = cen * rs
+        rs_ref[p : p + 1, :] = rs
+
+    todo = [(2, 0), (0, 1), (1, 1), (3, 0), (0, 2), (2, 1), (1, 2)]
+    for p in range(16):
+        norm_block(p)
+        if p % 2 == 1 and todo:
+            gat.advance(*todo.pop(0))
+    for step in todo:
+        gat.advance(*step)
+    for cp in own:
+        cp.wait()
+    for k in (4, 5, 6):
+        gat.start(k, 0)
+    gat.advance(0, 3)
+    for zz in range(4):
+        total = jnp.sum(wqb[zz, :, :, :, :, 0:128].astype(F32).reshape(8, 16, 128), axis=0)
+        par_ref[0:8, zz * 128 : (zz + 1) * 128] = total[0:8]
+        for k in range(4):
+            par_ref[8 + zz : 9 + zz, k * 128 : (k + 1) * 128] = total[8 + k : 9 + k]
+    par_ref[12:16, :] = jnp.zeros((4, 512), F32)
+    scr2 = par_ref[...].T
+    gains[0] = jnp.broadcast_to(scr2[:, 0:1], (512, 128))
+    gains[1] = jnp.broadcast_to(scr2[:, 1:2], (512, 128))
+    gains[2] = jnp.broadcast_to(scr2[:, 2:3], (512, 128))
+    gains[3] = jnp.broadcast_to(scr2[:, 3:4], (512, 128))
+
+    def finish_norm(p, carry):
+        cols = pl.ds(pl.multiple_of(p * 128, 128), 128)
+        n = ntf[:, cols]
+        normt_ref[:, cols] = (n * gains[0] + gains[1]).astype(BF)
+        nt_ref[:, cols] = n.astype(BF)
+        return carry
+
+    lax.fori_loop(0, 16, finish_norm, 0)
+
+    plan = [
+        [(2, 2), (3, 1), (1, 3)],
+        [(3, 2), (4, 0), (5, 0), ("s", 7)],
+        [(2, 3), (4, 1), (6, 0), ("s", 8)],
+        [(3, 3), (5, 1), (4, 2), (7, 0), ("s", 9)],
+        [(6, 1), (5, 2)],
+        [(7, 1), (8, 0), (4, 3)],
+        [(6, 2), (5, 3)],
+        [(8, 1), (9, 0)],
+        [(7, 2)],
+        [(9, 1), (6, 3)],
+        [(8, 2)],
+        [(7, 3)],
+    ]
+
+    def progress():
+        if plan:
+            for k, s in plan.pop(0):
+                if k == "s":
+                    gat.start(s, 0)
+                else:
+                    gat.advance(k, s)
+
+    saves = []
+    chs = []
+    for g in range(4):
+        w = wqb[:, :, :, :, :, 128 + g * 384 : 512 + g * 384].reshape(512, 384)
+        wt = w.astype(F32).T.astype(BF)
+        fs = slice(g * 128, (g + 1) * 128)
+        if g > 0:
+            saves[-1].wait()
+
+        def project(t, carry):
+            out = dot(wt, normt_ref[:, pl.ds(pl.multiple_of(t * 512, 512), 512)])
+            for k in range(4):
+                block = out[:, k * 128 : (k + 1) * 128]
+                block = jnp.concatenate(
+                    [block[0:128] + gains[2, fs, :], block[128:256], block[256:384] + gains[3, fs, :]],
+                    axis=0,
+                )
+                g_ref[pl.ds(t * 4 + k, 384, stride=16), :] = block.astype(BF).astype(F32)
+            return carry
+
+        lax.fori_loop(0, 4, project, 0)
+
+        def keep(i, carry):
+            rows = pl.ds(pl.multiple_of(i * 512, 512), 512)
+            qb[rows, :] = g_ref[rows, :].astype(BF)
+            return carry
+
+        lax.fori_loop(0, 12, keep, 0)
+        save = pltpu.make_async_copy(qb, qkv_save.at[g], lsem.at[g])
+        save.start()
+        saves.append(save)
+        progress()
+
+        def head(h, carry, g=g):
+            acc = pair_products(g_ref, h * 32, g_ref, 128 + h * 32)
+            bt = bt_ref[g * 4 + h]
+            s = [
+                acc[q] * SCALE + jnp.broadcast_to(bt[:, q : q + 1], (16, 128)) for q in range(16)
+            ]
+            m = tree(s, jnp.maximum)
+            e = [jnp.exp(v - m) for v in s]
+            inv = 1.0 / tree(e)
+            low = []
+            for q in range(16):
+                a = e[q] * inv
+                a_ref[pl.ds(pl.multiple_of((g * 4 + h) * 256 + q * 16, 16), 16), :] = a
+                low.append(a.astype(BF).astype(F32))
+            weighted(low, g_ref, 256 + h * 32, ct_ref, h * 32, None)
+            return carry
+
+        lax.fori_loop(0, 2, head, 0)
+        progress()
+        lax.fori_loop(2, 4, head, 0)
+        asave = pltpu.make_async_copy(
+            a_ref.at[pl.ds(g * 1024, 1024), :], att_save.at[pl.ds(g * 1024, 1024), :], lsem.at[4 + g]
+        )
+        asave.start()
+        chs.append(asave)
+        for p in range(16):
+            block = ct_ref[pl.ds(p, 128, stride=16), :]
+            ctxt_ref[fs, p * 128 : (p + 1) * 128] = block.astype(BF)
+            turned = block.T
+            lo, hi = spots(p)
+            cs_ref[pl.ds(lo, 64, stride=32), :] = turned[0:64]
+            cs_ref[pl.ds(hi, 64, stride=32), :] = turned[64:128]
+        for b in range(8):
+            ctx_ref[b, 16:256, fs] = cs_ref[b * 256 : b * 256 + 240, :].astype(BF)
+            chalo[g, b] = cs_ref[b * 256 + 240 : b * 256 + 256, :].astype(BF)
+        send = remote(chalo.at[g], ctx_ref.at[:, 0:16, pl.ds(g * 128, 128)], hss.at[g], hrs.at[g], me.over_y)
+        send.start()
+        chs.append(send)
+        progress()
+    while plan:
+        progress()
+    gat.advance(8, 3)
+    gat.advance(9, 2)
+    gat.advance(9, 3)
+    saves[-1].wait()
+    for cp in chs:
+        cp.wait()
+    xhalo.wait_send()
+    gat.close()
+
+
+def k1_call(x, wq, wp, w1, w2, smalls, fb, bt):
+    S = jax.ShapeDtypeStruct
+    lead = (4, 2, 2, 2)
+    outs = [
+        (S((8, 256, 512), BF), VM),
+        (S(lead + (16, 1664), BF), VM),
+        (S(lead + (16, 512), BF), HB),
+        (S(lead + (16, 2048), BF), HB),
+        (S(lead + (64, 512), BF), HB),
+        (S((16, 512), F32), VM),
+        (S((4, 6144, 128), BF), HB),
+        (S((4096, 128), F32), HB),
+        (S((512, 2048), BF), VM),
+        (S((512, 2048), BF), VM),
+        (S((512, 2048), BF), VM),
+        (S((16, 128), F32), VM),
+    ]
+    V = pltpu.VMEM
+    return pl.pallas_call(
+        k1_body,
+        out_shape=[o[0] for o in outs],
+        in_specs=[VM, VM, HB, HB, HB] + [VM] * 10,
+        out_specs=[o[1] for o in outs],
+        scratch_shapes=[
+            V((4, 2048, 128), F32), V((512, 2048), F32), V((6144, 128), F32), V((2048, 128), F32),
+            V((2048, 128), F32), V((4096, 128), F32), V((6144, 128), BF), V((8, 16, 512), BF),
+            V((4, 8, 16, 128), BF), V((4, 512, 128), F32), V((16, 128), F32),
+            pltpu.SemaphoreType.DMA((10, 6)), pltpu.SemaphoreType.DMA((10, 6)),
+            pltpu.SemaphoreType.DMA((5,)), pltpu.SemaphoreType.DMA((5,)),
+            pltpu.SemaphoreType.DMA((8,)), pltpu.SemaphoreType.DMA((3,)),
+        ],
+        compiler_params=pltpu.CompilerParams(
+            collective_id=1, has_side_effects=True, vmem_limit_bytes=60 << 20
+        ),
+        name="gather_attend",
+    )(x, wq, wp, w1, w2, *smalls, fb, bt)
+
 
 HEADS = 16
 HEAD_DIM = 32
@@ -302,6 +684,223 @@
     )
 
 
+def per_device_fast(
+    inputs,
+    grad_mask,
+    cotangent,
+    ln1_gain,
+    ln1_bias,
+    w_qkv,
+    q_bias,
+    v_bias,
+    w_proj,
+    proj_bias,
+    ln2_gain,
+    ln2_bias,
+    w_fc1,
+    fc1_bias,
+    w_fc2,
+    fc2_bias,
+    pos_table,
+):
+    bt = (
+        jnp.dot(table_onehot(), pos_table, precision=highest)
+        .reshape(16, 16, 16)
+        .transpose(2, 0, 1)
+    )
+    smalls = [
+        v.reshape(1, 16)
+        for v in (ln1_gain, ln1_bias, q_bias, v_bias, proj_bias, ln2_gain, ln2_bias, fc2_bias)
+    ]
+    ctx, wqb, wpb, w1b, w2b, par, qs, asv, ctxt, normt, nt, rs = k1_call(
+        inputs.reshape(8, 256, 512), w_qkv, w_proj, w_fc1, w_fc2, smalls, fc1_bias.reshape(1, 64), bt
+    )
+    gain_one, bias_one, qbias_full, vbias_full, pbias_full, gain_two, bias_two, fc2b_full = (
+        par[i] for i in range(8)
+    )
+    fc1b_full = par[8:12].reshape(2048)
+    qkv_full = (
+        wqb.reshape(512, 1664)[:, 128:].reshape(512, 4, 3, 128).transpose(0, 2, 1, 3).reshape(512, 1536)
+    )
+    proj_full, fc1_full, fc2_full = wpb.reshape(512, 512), w1b.reshape(512, 2048), w2b.reshape(2048, 512)
+    clip_count, row_count, column_count, feature_width = inputs.shape
+    score_scale = 1.0 / math.sqrt(HEAD_DIM)
+    float_type = jnp.float32
+    half_type = jnp.bfloat16
+    ahead = from_behind(inputs[:, :SHIFT], "slab", -1)
+    window_rows = jnp.concatenate([inputs[:, SHIFT:], ahead], axis=1).astype(float_type)
+    normed, first_pull = jax.vjp(
+        normalize, window_rows, gain_one.astype(float_type), bias_one.astype(float_type)
+    )
+    windows = to_windows(jnp.roll(normed.astype(half_type), -SHIFT, axis=2))
+    window_count = windows.shape[0]
+    token_count = window_count * WIN * WIN
+    head_shape = (window_count, WIN * WIN, HEADS, HEAD_DIM)
+    flat_windows = windows.reshape(token_count, feature_width)
+    projected = jnp.dot(flat_windows, qkv_full, preferred_element_type=float_type)
+    query_heads = (
+        (projected[:, :feature_width] + qbias_full.astype(float_type))
+        .astype(half_type)
+        .reshape(head_shape)
+    )
+    key_heads = (
+        projected[:, feature_width : 2 * feature_width].astype(half_type).reshape(head_shape)
+    )
+    value_heads = (
+        (projected[:, 2 * feature_width :] + vbias_full.astype(float_type))
+        .astype(half_type)
+        .reshape(head_shape)
+    )
+    onehot = table_onehot()
+    position_bias = (
+        jnp.dot(onehot, pos_table, precision=highest)
+        .reshape(WIN * WIN, WIN * WIN, HEADS)
+        .transpose(2, 0, 1)
+    )
+    scores = (
+        jnp.einsum("wqhc,wkhc->whqk", query_heads, key_heads, preferred_element_type=float_type)
+        * score_scale
+        + position_bias[None]
+    )
+    attention = jax.nn.softmax(scores, axis=-1)
+    attention_low = attention.astype(half_type)
+    context = jnp.einsum(
+        "whqk,wkhc->wqhc", attention_low, value_heads, preferred_element_type=float_type
+    )
+    context = context.astype(half_type).reshape(window_count, WIN * WIN, feature_width)
+    context_grid = jnp.roll(
+        from_windows(context, clip_count, row_count, column_count), SHIFT, axis=2
+    )
+    returned = from_behind(context_grid[:, row_count - SHIFT :], "slab", 1)
+    own_flat = jnp.concatenate([returned, context_grid[:, : row_count - SHIFT]], axis=1).reshape(
+        -1, feature_width
+    )
+    own_flat = ctx.reshape(-1, feature_width)
+    input_flat = inputs.reshape(-1, feature_width).astype(float_type)
+    middle = (
+        input_flat
+        + jnp.dot(own_flat, proj_full, preferred_element_type=float_type)
+        + pbias_full.astype(float_type)
+    )
+    second, second_pull = jax.vjp(
+        normalize, middle, gain_two.astype(float_type), bias_two.astype(float_type)
+    )
+    second_low = second.astype(half_type)
+    pre_act = jnp.dot(second_low, fc1_full, preferred_element_type=float_type) + fc1b_full.astype(
+        float_type
+    )
+    hidden, gelu_pull = jax.vjp(exact_gelu, pre_act)
+    hidden_low = hidden.astype(half_type)
+    output = (
+        middle
+        + jnp.dot(hidden_low, fc2_full, preferred_element_type=float_type)
+        + fc2b_full.astype(float_type)
+    )
+    incoming = (cotangent.astype(float_type) * grad_mask.astype(float_type)[..., None]).reshape(
+        -1, feature_width
+    )
+    incoming_low = incoming.astype(half_type)
+    fc2_grad = outer_sum(hidden_low, incoming_low)
+    fc2b_grad = jnp.sum(incoming, axis=0)
+    hidden_grad = times_transposed(incoming_low, fc2_full)
+    pre_grad = gelu_pull(hidden_grad)[0].astype(half_type)
+    fc1_grad = outer_sum(second_low, pre_grad)
+    fc1b_grad = jnp.sum(pre_grad.astype(float_type), axis=0)
+    second_grad = times_transposed(pre_grad, fc1_full)
+    middle_part, gain_two_grad, bias_two_grad = second_pull(second_grad)
+    middle_grad = incoming + middle_part
+    branch_low = middle_grad.astype(half_type)
+    proj_grad = outer_sum(own_flat, branch_low)
+    pbias_grad = jnp.sum(branch_low.astype(float_type), axis=0)
+    context_grad = (
+        times_transposed(branch_low, proj_full)
+        .astype(half_type)
+        .reshape(clip_count, row_count, column_count, feature_width)
+    )
+    sent_back = from_behind(context_grad[:, :SHIFT], "slab", -1)
+    window_context_grad = jnp.concatenate([context_grad[:, SHIFT:], sent_back], axis=1)
+    context_heads = to_windows(jnp.roll(window_context_grad, -SHIFT, axis=2)).reshape(head_shape)
+    value_grad = jnp.einsum(
+        "whqk,wqhc->wkhc", attention_low, context_heads, preferred_element_type=float_type
+    ).astype(half_type)
+    attention_grad = jnp.einsum(
+        "wqhc,wkhc->whqk", context_heads, value_heads, preferred_element_type=float_type
+    )
+    score_grad = (
+        attention * (attention_grad - jnp.sum(attention_grad * attention, -1, keepdims=True))
+    ).astype(half_type)
+    bias_cells = (
+        jnp.sum(score_grad.astype(float_type), axis=0)
+        .transpose(1, 2, 0)
+        .reshape(WIN * WIN * WIN * WIN, HEADS)
+    )
+    table_grad = lax.dot_general(onehot, bias_cells, (((0,), (0,)), ((), ())), precision=highest)
+    query_grad = (
+        jnp.einsum("whqk,wkhc->wqhc", score_grad, key_heads, preferred_element_type=float_type)
+        * score_scale
+    ).astype(half_type)
+    key_grad = (
+        jnp.einsum("whqk,wqhc->wkhc", score_grad, query_heads, preferred_element_type=float_type)
+        * score_scale
+    ).astype(half_type)
+    query_flat = query_grad.reshape(token_count, feature_width)
+    value_flat = value_grad.reshape(token_count, feature_width)
+    qkv_grad_low = jnp.concatenate(
+        [query_flat, key_grad.reshape(token_count, feature_width), value_flat], axis=1
+    )
+    qkv_grad = outer_sum(flat_windows, qkv_grad_low)
+    qbias_grad = jnp.sum(query_flat.astype(float_type), axis=0)
+    vbias_grad = jnp.sum(value_flat.astype(float_type), axis=0)
+    normed_grad = times_transposed(qkv_grad_low, qkv_full).reshape(
+        window_count, WIN * WIN, feature_width
+    )
+    normed_grid_grad = jnp.roll(
+        from_windows(normed_grad, clip_count, row_count, column_count), SHIFT, axis=2
+    )
+    rows_part, gain_one_grad, bias_one_grad = first_pull(normed_grid_grad)
+    halo_back = from_behind(
+        rows_part[:, row_count - SHIFT :].astype(jnp.bfloat16), "slab", 1
+    ).astype(jnp.float32)
+    input_grad = middle_grad.reshape(
+        clip_count, row_count, column_count, feature_width
+    ) + jnp.concatenate([halo_back, rows_part[:, : row_count - SHIFT]], axis=1)
+    shares = (
+        lax.psum_scatter(gain_one_grad, ("clip", "slab"), scatter_dimension=0, tiled=True),
+        lax.psum_scatter(bias_one_grad, ("clip", "slab"), scatter_dimension=0, tiled=True),
+        lax.psum_scatter(qkv_grad, ("clip", "slab"), scatter_dimension=0, tiled=True),
+        lax.psum_scatter(qbias_grad, ("clip", "slab"), scatter_dimension=0, tiled=True),
+        lax.psum_scatter(vbias_grad, ("clip", "slab"), scatter_dimension=0, tiled=True),
+        lax.psum_scatter(proj_grad, ("clip", "slab"), scatter_dimension=0, tiled=True),
+        lax.psum_scatter(pbias_grad, ("clip", "slab"), scatter_dimension=0, tiled=True),
+        lax.psum_scatter(gain_two_grad, ("clip", "slab"), scatter_dimension=0, tiled=True),
+        lax.psum_scatter(bias_two_grad, ("clip", "slab"), scatter_dimension=0, tiled=True),
+        lax.psum_scatter(fc1_grad, ("clip", "slab"), scatter_dimension=0, tiled=True),
+        lax.psum_scatter(fc1b_grad, ("clip", "slab"), scatter_dimension=0, tiled=True),
+        lax.psum_scatter(fc2_grad, ("clip", "slab"), scatter_dimension=0, tiled=True),
+        lax.psum_scatter(fc2b_grad, ("clip", "slab"), scatter_dimension=0, tiled=True),
+    )
+    table_total = lax.psum(table_grad, ("clip", "slab"))
+    output = output.reshape(clip_count, row_count, column_count, feature_width).astype(half_type)
+    return (
+        output,
+        input_grad.astype(half_type),
+        shares[0],
+        shares[1],
+        shares[2],
+        shares[3],
+        shares[4],
+        shares[5],
+        shares[6],
+        shares[7],
+        shares[8],
+        shares[9],
+        shares[10],
+        shares[11],
+        shares[12],
+        table_total,
+    )
+
+
 def solution(mesh):
     in_specs = (
         P("clip", "slab", None, None),
@@ -340,6 +939,7 @@
         P(("clip", "slab")),
         P(),
     )
+    fits = mesh.shape["clip"] == 16 and mesh.shape["slab"] == 2
     return jax.shard_map(
-        per_device, mesh=mesh, in_specs=in_specs, out_specs=out_specs, check_vma=False
-    )
+        per_device_fast if fits else per_device, mesh=mesh, in_specs=in_specs, out_specs=out_specs, check_vma=False
+    )

time: 917 us -> 851 us (0.928)
  blocking collectives: 146 us -> 41.6 us
  Pallas kernels: 0 us -> 69.4 us
  waiting for transfers between devices: 266 us -> 235 us
  local copies, waits for them, and re-layouts: 184 us -> 197 us
  matrix products: 217 us -> 205 us
    pallas_call x0 -> x1, Pallas kernels: none -> 69.4 us  [k1_call(): pl.pallas_call(k1_body, out_shape=[o[0] for o in outs], in_specs=[VM, VM,...]
    all_gather x1 -> x0, blocking collectives: 68.3 us -> none  [per_device(): lax.all_gather(w_proj, ('clip', 'slab'), axis=0, tiled=True)]
    concatenate x3 -> x7, local copies, waits for them, and re-layouts: 0.84 us -> 42.3 us  [the longest x6 41.4 us: per_device_fast(): jnp.concatenate([query_flat, key_grad.reshape(token_count, feature_width)...]
    unnamed x2 -> x1, blocking collectives: 77.7 us -> 41.6 us
    reduce_scatter x4, waiting for transfers between devices: 264 us -> 235 us  [the longest x1 141 us: per_device_fast(): lax.psum_scatter(fc2_grad, ('clip', 'slab'), scatter_dimension=0, tiled=T...]
    another operation x4 -> x2, local copies, waits for them, and re-layouts: 24.5 us -> 8.69 us  [the longest x1 6.67 us: per_device_fast(): to_windows(jnp.roll(window_context_grad, -SHIFT, axis=2))]
    dot_general x12 -> x11, matrix products: 150 us -> 137 us  [the longest x1 43.7 us: per_device_fast(): jnp.dot(second_low, fc1_full, preferred_element_type=float_type)]
    convert_element_type x5 -> x4, local copies, waits for them, and re-layouts: 43.6 us -> 32.6 us  [the longest x1 10.8 us: per_device_fast(): key_grad = (jnp.einsum('whqk,wqhc->wkhc', score_grad, query_heads, prefer...]
  transfers between devices with their start and end apart: 11 -> 7, of which waited for: 3 -> 2; matrix products, arithmetic and copies ran while one was open for 47% -> 55% of each run, Pallas kernels for 0% -> 8%
where the time goes in v1:
time: 851 us; the launch traced here: 844 us
  waiting for transfers between devices  235 us (28%)
  matrix products  205 us (24%)
  local copies, waits for them, and re-layouts  197 us (23%)
  other arithmetic  75.2 us (9%)
  Pallas kernels  69.4 us (8%)
  blocking collectives  41.6 us (5%)
  between operations  14.9 us (2%)
    reduce_scatter x1, waiting for transfers between devices, per_device_fast(): lax.psum_scatter(fc2_grad, ('clip', 'slab'), scatter_dimension=0, tiled=T...  141 us
    reduce_scatter x1, waiting for transfers between devices, per_device_fast(): lax.psum_scatter(fc1_grad, ('clip', 'slab'), scatter_dimension=0, tiled=T...  93.2 us
    pallas_call x1, Pallas kernels, k1_call(): pl.pallas_call(k1_body, out_shape=[o[0] for o in outs], in_specs=[VM, VM,...  69.4 us
    dot_general x1, matrix products, per_device_fast(): jnp.dot(second_low, fc1_full, preferred_element_type=float_type)  43.7 us
    unnamed x1, blocking collectives  41.6 us
    concatenate x6, local copies, waits for them, and re-layouts, per_device_fast(): jnp.concatenate([query_flat, key_grad.reshape(token_count, feature_width)...  41.4 us
    dot_general x4, matrix products, times_transposed(): lax.dot_general(left, right, (((1,), (1,)), ((), ())), preferred_element_...  36.8 us
    dot_general x4, matrix products, outer_sum(): lax.dot_general(left, right, (((0,), (0,)), ((), ())), preferred_element_...  31.5 us
  transfers between devices with their start and end apart: 7, of which 2 were waited for; matrix products, arithmetic and copies ran while one was open for 55% of the time, Pallas kernels for 8%

profile of v1, /device:TPU:0, one launch (start us, length us, event | category | flops | bytes accessed | tf_op | source)
XLA Modules:
  0.0 843.6 jit_solution(2925568599195797988)
XLA Ops:
  8.9 3.0 collective-permute-start
  13.1 69.4 %gather_attend.1 = (bf16[8,256,512]{2,1,0:T(8,128)(2,1)}, bf16[4,2,2,2,16,1664]{5,4,3,2,1,0:T(8,128)(2,1)}, bf16[4,2,2,2,16,512]{5,4,3,2,1,0:T(8,128)(2,1)}, bf1...) custom-call(bf16[8,256,512]{2,1,0:T(8,128)(2,1)} %bitcast.100, ...), custom_call_target="tpu_custom_call" | custom-call | tf_op jit(solution)/shard_map/gather_attend/pallas_call | solution.py:370
  84.8 3.9 fusion.82
  91.9 4.3 fusion.62
  97.0 43.7 %multiply_convert_fusion.3 = (bf16[2048,2048]{1,0:T(8,128)(2,1)}, f32[2048,2048]{1,0:T(8,128)}, f32[2048,2048]{1,0:T(8,128)}) fusion(f32[2048]{0:T(1024)S(1)} %bitcast.124, bf16[512,2048]{1,0:T(8,128)(2,1)S(1)} %bitcast.146, f32[2048,512]{1,0:T(8,128)S(1)} %copy-done.7, f32[512]{0:T(512)S(1)} %bitcast.131, f32[512]{0:T(512)S(1)} %bitcast.126, ...), kind=kOutput, calls=%fused_computation.14 | convolution fusion | flops 4577034240 | bytes 48263168 | tf_op jit(solution)/shard_map/dot_general | solution.py:789
  140.7 20.1 %convert_reduce_fusion.1 = (f32[2048]{0:T(1024)}, bf16[2048,2048]{1,0:T(8,128)(2,1)}) fusion(f32[2048,2048]{1,0:T(8,128)} %get-tuple-element.114, bf16[2048,512]{1,0:T(8,128)(2,1)S(1)} %bitcast.110, bf16[2048,512]{1,0:T(8,128)(2,1)} %bitcast.143, f32[2048,2048]{1,0:T(8,128)} %get-tuple-element.134, f32[2048]{0:T(1024)S(1)} %bitcast.125), kind=kOutput, calls=%fused_computation.4 | convolution fusion | flops 4366268416 | bytes 46153728 | tf_op jit(solution)/shard_map/dot_general | solution.py:451
  160.8 11.9 %multiply_reduce_fusion.1 = (f32[512]{0:T(512)}, f32[2048]{0:T(1024)S(1)}, f32[512]{0:T(512)}, f32[2048,512]{1,0:T(8,128)S(1)}) fusion(f32[2048,512]{1,0:T(8,128)} %copy-done.6, f32[2048]{0:T(1024)S(1)} %fusion.70, f32[2048]{0:T(1024)S(1)} %broadcast_multiply_fusion.1, f32[512]{0:T(512)S(1)} %bitcast.127, bf16[2048,2048]{1,0:T(8,128)(2,1)} %get-tuple-element.145, ...), kind=kOutput, calls=%fused_computation.85 | convolution fusion | flops 4303352832 | bytes 18905088 | tf_op jit(solution)/shard_map/dot_general | solution.py:451
  185.8 2.9 copy_dynamic-update-slice_fusion
  190.9 3.2 copy.162
  198.3 3.0 copy.134
  214.5 5.5 fusion.84
  220.7 3.3 fusion.54
  224.0 10.3 %reshape.312 = bf16[128,16,16,32]{3,2,1,0:T(8,128)(2,1)} reshape(bf16[2048,512]{1,0:T(8,128)(2,1)} %get-tuple-element.116) | data formatting | bytes 4194304 | tf_op jit(solution)/shard_map/reshape | solution.py:744
  234.3 7.0 reshape.311
  244.0 6.7 reshape_reshape.8
  250.6 10.4 %reshape.315 = bf16[128,16,16,32]{3,2,1,0:T(8,128)(2,1)} reshape(bf16[2048,512]{1,0:T(8,128)(2,1)} %get-tuple-element.115) | data formatting | bytes 4194304 | tf_op jit(solution)/shard_map/reshape | solution.py:752
  261.1 13.6 %fusion.14 = f32[128,16,16,16]{2,3,1,0:T(8,128)} fusion(bf16[128,16,16,32]{3,2,1,0:T(8,128)(2,1)} %reshape.311, bf16[128,16,16,32]{3,2,1,0:T(8,128)(2,1)} %reshape.312), kind=kOutput, calls=%fused_computation.37 | convolution fusion | flops 33554432 | bytes 6291456 | tf_op jit(solution)/shard_map/wqhc,wkhc->whqk/dot_general | solution.py:761
  274.7 25.2 %fusion.83 = (f32[128,16,16]{2,1,0:T(8,128)S(1)}, f32[128,16,16,16]{2,3,1,0:T(8,128)}) fusion(f32[128,16,16,16]{2,3,1,0:T(8,128)} %fusion.14, f32[16,16,16]{1,2,0:T(8,128)S(1)} %copy-done.28), kind=kOutput, calls=%fused_computation.141 | output fusion | flops 3145743 | bytes 4341760 | tf_op jit(solution)/shard_map/sub | solution.py:765
  299.9 14.2 %convert_reduce_fusion.2 = (f32[16,32]{1,0:T(8,128)}, bf16[128,16,16,32]{3,1,2,0:T(8,128)(2,1)}) fusion(bf16[128,16,16,32]{3,2,1,0:T(8,128)(2,1)} %reshape_reshape.8, f32[128,16,16,16]{2,3,1,0:T(8,128)} %get-tuple-element.137, f32[128,16,16]{2,1,0:T(8,128)S(1)} %get-tuple-element.136), kind=kOutput, calls=%fused_computation.5 | convolution fusion | flops 37748224 | bytes 6424576 | tf_op jit(solution)/shard_map/whqk,wqhc->wkhc/dot_general | solution.py:823
  314.1 20.4 %multiply_reduce_fusion = (f32[128,16,16]{2,1,0:T(8,128)S(1)}, f32[128,16,16,16]{2,3,1,0:T(8,128)}) fusion(f32[128,16,16,16]{2,3,1,0:T(8,128)} %get-tuple-element.137, f32[128,16,16]{2,1,0:T(8,128)S(1)} %get-tuple-element.136, bf16[128,16,16,32]{3,2,1,0:T(8,128)(2,1)} %reshape.315, bf16[128,16,16,32]{3,2,1,0:T(8,128)(2,1)} %reshape_reshape.8), kind=kOutput, calls=%fused_computation.10 | convolution fusion | flops 35094528 | bytes 8650752 | tf_op jit(solution)/shard_map/wqhc,wkhc->whqk/dot_general | solution.py:826
  334.5 15.4 %convert_reduce_fusion = (f32[16,16,16]{1,2,0:T(8,128)S(1)}, bf16[128,16,16,16]{2,3,1,0:T(8,128)(2,1)}) fusion(f32[128,16,16,16]{2,3,1,0:T(8,128)} %get-tuple-element.139, f32[128,16,16]{2,1,0:T(8,128)S(1)} %get-tuple-element.138, f32[128,16,16,16]{2,3,1,0:T(8,128)} %get-tuple-element.137, f32[128,16,16]{2,1,0:T(8,128)S(1)} %get-tuple-element.136), kind=kLoop, calls=%fused_computation.3 | loop fusion | flops 3141632 | bytes 5521408 | tf_op jit(solution)/shard_map/reduce_sum | solution.py:833
  349.9 10.1 %convert_reduce_fusion.3 = (f32[16,32]{1,0:T(8,128)S(1)}, bf16[128,16,16,32]{3,1,2,0:T(8,128)(2,1)}) fusion(bf16[128,16,16,16]{2,3,1,0:T(8,128)(2,1)} %get-tuple-element.108, bf16[128,16,16,32]{3,2,1,0:T(8,128)(2,1)} %reshape.311), kind=kOutput, calls=%fused_computation.6 | convolution fusion | flops 37748224 | bytes 5244928 | tf_op jit(solution)/shard_map/whqk,wkhc->wqhc/dot_general | solution.py:839
  360.0 10.8 %copy.145 = bf16[128,16,16,32]{3,2,1,0:T(8,128)(2,1)} copy(bf16[128,16,16,32]{3,1,2,0:T(8,128)(2,1)} %get-tuple-element.141) | data formatting | bytes 4194304 | tf_op jit(solution)/shard_map/convert_element_type | solution.py:841
  370.9 11.1 %reshape.317 = bf16[2048,512]{1,0:T(8,128)(2,1)S(1)} reshape(bf16[128,16,16,32]{3,2,1,0:T(8,128)(2,1)} %copy.145) | data formatting | bytes 4194304 | tf_op jit(solution)/shard_map/reshape | solution.py:846
  381.9 13.5 %fusion.40 = bf16[128,16,16,32]{3,1,2,0:T(8,128)(2,1)} fusion(bf16[128,16,16,16]{2,3,1,0:T(8,128)(2,1)} %get-tuple-element.108, bf16[128,16,16,32]{3,2,1,0:T(8,128)(2,1)} %reshape.312), kind=kOutput, calls=%fused_computation.59 | convolution fusion | flops 35651584 | bytes 5242880 | tf_op jit(solution)/shard_map/whqk,wqhc->wkhc/dot_general | solution.py:843
  395.4 10.8 %copy.147 = bf16[128,16,16,32]{3,2,1,0:T(8,128)(2,1)} copy(bf16[128,16,16,32]{3,1,2,0:T(8,128)(2,1)} %fusion.40) | data formatting | bytes 4194304 | tf_op jit(solution)/shard_map/convert_element_type | solution.py:845
  406.3 12.2 %reshape.318 = bf16[2048,512]{1,0:T(8,128)(2,1)} reshape(bf16[128,16,16,32]{3,2,1,0:T(8,128)(2,1)} %copy.147) | data formatting | bytes 4194304 | tf_op jit(solution)/shard_map/reshape | solution.py:849
  418.5 10.8 %copy.149 = bf16[128,16,16,32]{3,2,1,0:T(8,128)(2,1)} copy(bf16[128,16,16,32]{3,1,2,0:T(8,128)(2,1)} %get-tuple-element.143) | data formatting | bytes 4194304 | tf_op jit(solution)/shard_map/convert_element_type | solution.py:825
  429.3 12.0 %reshape.319 = bf16[2048,512]{1,0:T(8,128)(2,1)} reshape(bf16[128,16,16,32]{3,2,1,0:T(8,128)(2,1)} %copy.149) | data formatting | bytes 4194304 | tf_op jit(solution)/shard_map/reshape | solution.py:847
  441.3 8.0 fusion.31
  449.4 11.4 %fusion.77 = f32[512,2048]{1,0:T(8,128)} fusion(bf16[2048,2048]{1,0:T(8,128)(2,1)} %get-tuple-element.145, f32[2048,512]{1,0:T(8,128)} %copy-done.6, f32[512]{0:T(512)S(1)} %bitcast.132, f32[512]{0:T(512)S(1)} %bitcast.129, f32[2048]{0:T(1024)S(1)} %copy-done.37, f32[2048]{0:T(1024)S(1)} %copy-done.32), kind=kOutput, calls=%fused_computation.136 | convolution fusion | flops 4300210176 | bytes 16797696 | tf_op jit(solution)/shard_map/dot_general | solution.py:457
  461.3 2.5 bitcast_convert_fusion
  463.8 9.9 %fusion.85 = f32[2048,512]{1,0:T(8,128)} fusion(bf16[2048,2048]{1,0:T(8,128)(2,1)} %get-tuple-element.113, bf16[2048,512]{1,0:T(8,128)(2,1)S(1)} %bitcast_convert_fusion), kind=kOutput, calls=%fused_computation.143 | convolution fusion | flops 4294967296 | bytes 14680064 | tf_op jit(solution)/shard_map/dot_general | solution.py:457
  476.7 11.3 %add_convert_fusion.1 = bf16[2048,512]{1,0:T(8,128)(2,1)} fusion(f32[2048,512]{1,0:T(8,128)} %copy-done.6, bf16[2048,2048]{1,0:T(8,128)(2,1)} %get-tuple-element.113, bf16[2048,512]{1,0:T(8,128)(2,1)} %bitcast.144, f32[512]{0:T(512)S(1)} %bitcast.130), kind=kOutput, calls=%fused_computation.89 | convolution fusion | flops 4298113024 | bytes 16779264 | tf_op jit(solution)/shard_map/dot_general | solution.py:796
  488.0 10.8 %concatenate.36 = bf16[8,8,2,4,4,512]{5,4,3,2,1,0:T(4,128)(2,1)S(1)} reshape(bf16[128,16,16,32]{3,2,1,0:T(8,128)(2,1)} %copy.145) | data formatting | bytes 4194304 | tf_op jit(solution)/shard_map/concatenate | solution.py:848
  498.7 11.7 %concatenate.37 = bf16[8,8,2,4,4,512]{5,4,3,2,1,0:T(4,128)(2,1)} reshape(bf16[128,16,16,32]{3,2,1,0:T(8,128)(2,1)} %copy.147) | data formatting | bytes 4194304 | tf_op jit(solution)/shard_map/concatenate | solution.py:848
  510.5 11.9 %concatenate.38 = bf16[8,8,2,4,4,512]{5,4,3,2,1,0:T(4,128)(2,1)} reshape(bf16[128,16,16,32]{3,2,1,0:T(8,128)(2,1)} %copy.149) | data formatting | bytes 4194304 | tf_op jit(solution)/shard_map/concatenate | solution.py:848
  522.4 2.4 copy.150
  524.8 2.3 copy.151
  527.1 2.3 copy.152
  529.4 3.4 fusion.58
  532.9 2.6 copy.153
  538.9 3.0 fusion.51
  542.0 2.3 broadcast_add_fusion
  547.4 41.6 %all-reduce.9 = (f32[512]{0:T(512)S(1)}, f32[512]{0:T(512)S(1)}, f32[512]{0:T(512)S(1)}, f32[512]{0:T(512)S(1)}, f32[512]{0:T(512)S(1)}, /*index=5*/f32[512]{0:T...) all-reduce(f32[512]{0:T(512)S(1)} %get-tuple-element.94, ...), channel_id=2, replica_groups=mesh['clip'=16,'slab'=2] {'clip','slab'}, use_global_device_ids=true, to_apply=%region_12.13.clone | all-reduce | flops 6928 | bytes 55424
  594.3 5.9 fusion.56
  602.2 93.2 %reduce-scatter.9.cloned.1.call-done = f32[16,2048]{1,0:T(8,128)} async-done(((f32[512,2048]{1,0:T(8,128)}), f32[16,2048]{1,0:T(8,128)}) %reduce-scatter.9.cloned.1.call-update) | async-done | bytes 131088 | tf_op jit(solution)/shard_map/reduce_scatter | solution.py:877
  695.5 141.4 %reduce-scatter.11.cloned.1.call-done = f32[64,512]{1,0:T(8,128)} async-done(((f32[2048,512]{1,0:T(8,128)}), f32[64,512]{1,0:T(8,128)}) %reduce-scatter.11.cloned.1.call-update) | async-done | bytes 131088 | tf_op jit(solution)/shard_map/reduce_scatter | solution.py:879
  (195 shorter events, 62.0 us)
Async XLA Ops:
  7.2 4.9 copy-start
  7.2 595.0 %reduce-scatter.7.cloned.1.call-start = ((), (), s32[]{:S(2)}) async-start(), calls=%async_computation.5 | async-start | bytes 1081344 | tf_op jit(solution)/shard_map/reduce_scatter | solution.py:873
  8.9 194.1 %collective-permute-start = (bf16[8,2,8,512]{3,0,2,1:T(8,128)(2,1)}, bf16[8,2,8,512]{3,0,2,1:T(8,128)(2,1)}, u32[]{:S(2)}, u32[]{:S(2)}) collective-permute-start(bf16[8,2,8,512]{3,0,2,1:T(8,128)(2,1)} %copy.163), channel_id=1, source_target_pairs={{1,0},{0,1},{3,2},{2,3},{5,4},{4,5},{7,6},{6,7},{9,8},{8,9},{11,10... | collective-permute-start | bytes 393224 | tf_op jit(solution)/shard_map/ppermute | solution.py:404
  12.0 72.8 %copy-start.52 = (s32[256]{0:T(256)}, s32[256]{0:T(256)S(1)}, u32[]{:S(2)}) copy-start(s32[256]{0:T(256)S(1)} %reshape.324) | copy-start | bytes 3076
  84.1 12.1 %copy-start.50 = (f32[1,512]{1,0:T(1,128)}, f32[1,512]{1,0:T(1,128)S(1)}, u32[]{:S(2)}) copy-start(f32[1,512]{1,0:T(1,128)S(1)} %get-tuple-element.129) | copy-start | bytes 6148
  84.1 88.7 %copy-start.45 = (f32[1,512]{1,0:T(1,128)}, f32[1,512]{1,0:T(1,128)S(1)}, u32[]{:S(2)}) copy-start(f32[1,512]{1,0:T(1,128)S(1)} %get-tuple-element.130) | copy-start | bytes 6148
  88.7 3.0 copy-start.35
  88.7 3.1 copy-start.20
  88.8 84.0 %copy-start.31 = (f32[2048]{0:T(1024)}, f32[2048]{0:T(1024)S(1)}, u32[]{:S(2)}) copy-start(f32[2048]{0:T(1024)S(1)} %broadcast_multiply_fusion.1) | copy-start | bytes 24580
  91.7 4.5 copy-start.29
  91.8 81.0 %copy-start.36 = (f32[2048]{0:T(1024)}, f32[2048]{0:T(1024)S(1)}, u32[]{:S(2)}) copy-start(f32[2048]{0:T(1024)S(1)} %fusion.70) | copy-start | bytes 24580
  91.9 4.3 copy-start.7
  91.9 5.1 copy-start.54
  97.0 43.7 %copy-start.22 = (bf16[8,32,8,512]{3,2,1,0:T(8,128)(2,1)S(1)}, bf16[8,32,8,512]{3,2,1,0:T(8,128)(2,1)}, u32[]{:S(2)}) copy-start(bf16[8,32,8,512]{3,2,1,0:T(8,128)(2,1)} %get-tuple-element.122) | copy-start | bytes 6291460
  160.8 12.0 %copy-start.30 = (f32[2048]{0:T(1024)S(1)}, f32[2048]{0:T(1024)}, u32[]{:S(2)}) copy-start(f32[2048]{0:T(1024)} %copy-done.29) | copy-start | bytes 24580
  160.8 12.0 %copy-start.8 = (f32[2048,512]{1,0:T(8,128)S(1)}, f32[2048,512]{1,0:T(8,128)}, u32[]{:S(2)}) copy-start(f32[2048,512]{1,0:T(8,128)} %copy-done.6) | copy-start | bytes 12582916
  176.1 5.5 copy-start.4
  176.1 5.5 copy-start.21
  179.5 29.5 %collective-permute-start.1 = (bf16[8,2,8,512]{3,0,2,1:T(8,128)(2,1)}, bf16[8,2,8,512]{3,0,2,1:T(8,128)(2,1)}, u32[]{:S(2)}, u32[]{:S(2)}) collective-permute-start(bf16[8,2,8,512]{3,0,2,1:T(8,128)(2,1)} %copy.166), channel_id=1, source_target_pairs={{1,0},{0,1},{3,2},{2,3},{5,4},{4,5},{7,6},{6,7},{9,8},{8,9},{11,10... | collective-permute-start | bytes 393224 | tf_op jit(solution)/shard_map/ppermute | solution.py:404
  183.9 4.8 copy-start.13
  183.9 418.3 %reduce-scatter.5.cloned.1.call-start = ((), (), s32[]{:S(2)}) async-start(), calls=%async_computation.4 | async-start | bytes 3244032 | tf_op jit(solution)/shard_map/reduce_scatter | solution.py:870
  185.8 4.4 copy-start.26
  194.1 12.7 %copy-start.2 = (bf16[8,30,8,512]{3,0,2,1:T(8,128)(2,1)}, bf16[8,30,8,512]{3,0,2,1:T(8,128)(2,1)S(1)}, u32[]{:S(2)}) copy-start(bf16[8,30,8,512]{3,0,2,1:T(8,128)(2,1)S(1)} %copy.162) | copy-start | bytes 5898244
  201.3 7.4 copy-start.9
  201.3 5.5 copy-start.33
  201.3 5.5 copy-start.38
  204.3 4.6 copy-start.16
  206.2 2.7 copy-start.18
  261.1 13.6 %copy-start.28 = (f32[16,16,16]{1,2,0:T(8,128)S(1)}, f32[16,16,16]{1,2,0:T(8,128)}, u32[]{:S(2)}) copy-start(f32[16,16,16]{1,2,0:T(8,128)} %copy.137) | copy-start | bytes 49156
  441.3 8.0 copy-start.32
  441.3 8.1 copy-start.37
  441.3 8.1 copy-start.46
  441.3 8.1 copy-start.51
  449.3 246.1 %reduce-scatter.9.cloned.1.call-start = ((), (), s32[]{:S(2)}) async-start(), calls=%async_computation.6 | async-start | bytes 4325376 | tf_op jit(solution)/shard_map/reduce_scatter | solution.py:877
  460.8 376.1 %reduce-scatter.11.cloned.1.call-start = ((), (), s32[]{:S(2)}) async-start(), calls=%async_computation.7 | async-start | bytes 4325376 | tf_op jit(solution)/shard_map/reduce_scatter | solution.py:879
  473.8 2.9 copy-start.49
  522.4 4.7 copy-start.12
  524.8 4.7 copy-start.23
  536.3 2.7 copy-start.19
  544.3 2.7 copy-start.43
  544.3 2.8 copy-start.53
  544.4 3.0 copy-start.39
  544.4 3.0 copy-start.40
  544.4 3.0 copy-start.44
  544.4 3.0 copy-start.47
  544.4 3.0 copy-start.48
  547.1 47.2 %collective-permute-start.2 = (bf16[8,2,8,512]{3,0,2,1:T(8,128)(2,1)S(1)}, bf16[8,2,8,512]{3,0,2,1:T(8,128)(2,1)S(1)}, u32[]{:S(2)}, u32[]{:S(2)}) collective-permute-start(bf16[8,2,8,512]{3,0,2,1:T(8,128)(2,1)S(1)} %slice.132), channel_id=1, source_target_pairs={{1,0},{0,1},{3,2},{2,3},{5,4},{4,5},{7,6},{6,7},{9,8},{8,9},{11,10... | collective-permute-start | bytes 393224 | tf_op jit(solution)/shard_map/ppermute | solution.py:404
  594.3 242.6 %copy-start.1 = (f32[49,16]{0,1:T(8,128)S(1)}, f32[49,16]{0,1:T(8,128)}, u32[]{:S(2)}) copy-start(f32[49,16]{0,1:T(8,128)} %param.33) | copy-start | bytes 9412
  (14 other events, 22.0 us)
Sparse Core Ops, SparseCore 0:
  184.0 135.0 reduce-scatter.6
  449.4 101.8 reduce-scatter.4
  554.3 141.1 reduce-scatter.8
  698.3 138.5 reduce-scatter.10

commit v2 on v1

--- a/solution.py
+++ b/solution.py
@@ -385,6 +385,518 @@
         ),
         name="gather_attend",
     )(x, wq, wp, w1, w2, *smalls, fb, bt)
+
+
+def gelu_parts(a):
+    z = jnp.abs(a) * 0.7071067811865476
+    t = 1.0 / (1.0 + 0.3275911 * z)
+    e = jnp.exp(a * a * -0.5)
+    p = 0.5307027145 * t - 0.7265760135
+    p = p * t + 0.7107068705
+    p = p * t - 0.142248368
+    p = p * t + 0.127414796
+    tail = p * t * e
+    return jnp.where(a >= 0, 1.0 - tail, tail), e * 0.3989422804014327
+
+
+CH = 512
+FJ = 512
+
+
+def k2_body(
+    x_ref, ctx_ref, cot_ref, mask_ref, par_ref, wp_ref, w1_ref, w2_ref,
+    out_ref, mg_ref, br_ref, g1_ref, g2_ref, small_ref, hid_ref, pg_ref, sec_ref, inc_ref,
+):
+    pb, g2, b2, fb2 = (par_ref[k : k + 1, :] for k in (4, 5, 6, 7))
+    small_ref[...] = jnp.zeros_like(small_ref)
+    rsel = (
+        lax.broadcasted_iota(jnp.int32, (256, 32), 0) // 8
+        == lax.broadcasted_iota(jnp.int32, (256, 32), 1)
+    ).astype(F32).astype(BF)
+    csel = lax.broadcasted_iota(jnp.int32, (256, 8), 0) % 8 == lax.broadcasted_iota(
+        jnp.int32, (256, 8), 1
+    )
+
+    def chunk(i, carry):
+        rows = pl.ds(pl.multiple_of(i * CH, CH), CH)
+        mid = x_ref[rows, :].astype(F32) + dot(ctx_ref[rows, :], wp_ref[...]) + pb
+        cen = mid - jnp.mean(mid, 1, keepdims=True)
+        rs = lax.rsqrt(jnp.mean(cen * cen, 1, keepdims=True) + 1e-6)
+        n2 = cen * rs
+        sec = (n2 * g2 + b2).astype(BF)
+        sec_ref[rows, :] = sec
+        marks = []
+        for k in range(CH // 256):
+            spread = dot(rsel, mask_ref[i * (CH // 256) + k].astype(F32).astype(BF))
+            marks.append(jnp.sum(jnp.where(csel, spread, 0.0), 1, keepdims=True))
+        inc = cot_ref[rows, :].astype(F32) * jnp.concatenate(marks, 0)
+        low = inc.astype(BF)
+        inc_ref[rows, :] = low
+        small_ref[7:8, :] += jnp.sum(inc, 0, keepdims=True)
+        total = back = None
+        for j in range(2048 // FJ):
+            cols = slice(j * FJ, (j + 1) * FJ)
+            pre = dot(sec, w1_ref[:, cols]) + par_ref[8 + j : 9 + j, :]
+            hg = dot(low, w2_ref[cols, :], NT)
+            cdf, pdf = gelu_parts(pre)
+            hid = (pre * cdf).astype(BF)
+            hid_ref[rows, cols] = hid
+            pg = (hg * (cdf + pre * pdf)).astype(BF)
+            pg_ref[rows, cols] = pg
+            small_ref[8 + j : 9 + j, :] += jnp.sum(pg.astype(F32), 0, keepdims=True)
+            o = dot(hid, w2_ref[cols, :])
+            s = dot(pg, w1_ref[:, cols], NT)
+            total = o if total is None else total + o
+            back = s if back is None else back + s
+        out_ref[rows, :] = (mid + total + fb2).astype(BF)
+        small_ref[5:6, :] += jnp.sum(back * n2, 0, keepdims=True)
+        small_ref[6:7, :] += jnp.sum(back, 0, keepdims=True)
+        eg = back * g2
+        r = (eg - jnp.mean(eg, 1, keepdims=True) - n2 * jnp.mean(eg * n2, 1, keepdims=True)) * rs
+        mg = inc + r
+        mg_ref[rows, :] = mg
+        br = mg.astype(BF)
+        br_ref[rows, :] = br
+        small_ref[4:5, :] += jnp.sum(br.astype(F32), 0, keepdims=True)
+        return carry
+
+    lax.fori_loop(0, 2048 // CH, chunk, 0)
+
+    def grads_one(j, carry):
+        cols = pl.ds(pl.multiple_of(j * 256, 256), 256)
+        g1_ref[:, cols] = dot(sec_ref[...], pg_ref[:, cols], TN).astype(BF)
+        return carry
+
+    lax.fori_loop(0, 8, grads_one, 0)
+
+    def grads_two(j, carry):
+        cols = pl.ds(pl.multiple_of(j * 256, 256), 256)
+        g2_ref[cols, :] = dot(hid_ref[:, cols], inc_ref[...], TN).astype(BF)
+        return carry
+
+    lax.fori_loop(0, 8, grads_two, 0)
+
+
+def k2_call(x, ctx, cot, mask, par, wp, w1, w2):
+    S = jax.ShapeDtypeStruct
+    V = pltpu.VMEM
+    return pl.pallas_call(
+        k2_body,
+        out_shape=[
+            S((2048, 512), BF), S((2048, 512), F32), S((2048, 512), BF),
+            S((512, 2048), BF), S((2048, 512), BF), S((16, 512), F32),
+        ],
+        in_specs=[VM] * 8,
+        out_specs=[VM] * 6,
+        scratch_shapes=[V((2048, 2048), BF)] * 2 + [V((2048, 512), BF)] * 2,
+        compiler_params=pltpu.CompilerParams(vmem_limit_bytes=60 << 20),
+        name="feed_forward",
+    )(x, ctx, cot, mask, par, wp, w1, w2)
+
+
+class Scatter:
+    def __init__(self, place, pieces, ssem, rsem):
+        self.me = place
+        self.pieces = pieces
+        self.steps = []
+        z, x, c, y = place.z, place.x, place.c, place.y
+        al = slice(None)
+        for k, (src, c0, n, first_y, own, s, r1, r2, r3, r4, done) in enumerate(pieces):
+            cols = pl.ds(c0, n)
+
+            def cp(a, b, i, to, k=k):
+                return remote(a, b, ssem.at[k, i], rsem.at[k, i], to)
+
+            steps = [[cp(src.at[:, :, 1 - c, :, :, cols], r1, 0, place.over_core)]]
+            if first_y:
+                steps.append([cp(s.at[:, :, 1 - y], r2, 1, place.over_y)])
+                steps.append([cp(s.at[:, 1 - x, y], r3, 2, place.over_x)])
+            else:
+                steps.append([cp(s.at[:, 1 - x], r2, 1, place.over_x)])
+                steps.append([cp(s.at[:, x, 1 - y], r3, 2, place.over_y)])
+            steps.append(
+                [
+                    cp(s.at[(z + 1 + d) % 4, x, y], r4.at[d], 3 + d, place.along_z[d])
+                    for d in range(3)
+                ]
+            )
+            self.steps.append(steps)
+
+    def start(self, k, i):
+        for copy in self.steps[k][i]:
+            copy.start()
+
+    def advance(self, k, i):
+        me = self.me
+        z, x, c, y = me.z, me.x, me.c, me.y
+        src, c0, n, first_y, own, s, r1, r2, r3, r4, done = self.pieces[k]
+        cols = pl.ds(c0, n)
+        for copy in self.steps[k][i]:
+            copy.wait_recv()
+        if i == 0:
+            if own is not None:
+                own.wait()
+
+            def add(zz, carry):
+                held = s[zz] if own is not None else src[zz, :, c, :, :, cols]
+                s[zz] = (held.astype(F32) + r1[zz].astype(F32)).astype(BF)
+                return carry
+
+            lax.fori_loop(0, 4, add, 0)
+        elif i == 1 and first_y:
+            s[:, :, y] = (s[:, :, y].astype(F32) + r2[...].astype(F32)).astype(BF)
+        elif i == 1:
+            s[:, x] = (s[:, x].astype(F32) + r2[...].astype(F32)).astype(BF)
+        elif i == 2:
+            s[:, x, y] = (s[:, x, y].astype(F32) + r3[...].astype(F32)).astype(BF)
+        else:
+            done(tree([s[z, x, y].astype(F32)] + [r4[d].astype(F32) for d in range(3)]))
+        if i < 3:
+            self.start(k, i + 1)
+
+    def close(self):
+        for steps in self.steps:
+            for step in steps:
+                for copy in step:
+                    copy.wait_send()
+
+
+def k3_body(
+    br_ref, mg_h, g1_ref, g2_ref, small_ref, wqb_h, wp_h, qkv_save, att_save, ctxt_h, normt_h, nt_h, rs_ref,
+    ig_ref, gq_ref, gp_ref, gf1_ref, gf2_ref, v0, v1, v2, v3, v4, v5, v6, v7, fb_ref, tab_ref,
+    bs, bp, mg, wq, wp, qb, g_ref, dg, dc, a_ref, dqt, ctxt, normt, nt, ds_ref, low_ref,
+    gacc, pgrad, qgrad, bhalo, rhalo, rout, cells, ar, arr, arz,
+    s4, r14, r24, r34, r44, sp, r1p, r2p, r3p, r4p, sq, r1q, r2q, r3q, r4q,
+    ssem, rsem, hss, hrs, lsem, asems, aremr,
+):
+    me = Place()
+    z, x, c, y = me.z, me.x, me.c, me.y
+    me.greet()
+
+    def local(src, dst, i):
+        cp = pltpu.make_async_copy(src, dst, lsem.at[i])
+        cp.start()
+        return cp
+
+    pieces = []
+    owns = []
+    for k, (src, rows, n) in enumerate(((g2_ref, 64, 256), (g1_ref, 16, 1024))):
+        for half in range(2):
+            j = k * 2 + half
+            own = local(
+                src.at[:, :, c, :, :, pl.ds(half * n, n)], s4[j], 10 + j
+            )
+            out = gf2_ref if k == 0 else gf1_ref
+
+            def done(v, out=out, c0=half * n, n=n):
+                out[:, c0 : c0 + n] = v
+
+            pieces.append((src, half * n, n, half == 0, own, s4[j], r14[j], r24[j], r34[j], r44[j], done))
+    for half in range(2):
+
+        def done(v, c0=half * 256):
+            gp_ref[:, c0 : c0 + 256] = v
+
+        pieces.append(
+            (pgrad, half * 256, 256, half == 0, None, sp.at[half], r1p.at[half], r2p.at[half], r3p.at[half], r4p.at[half], done)
+        )
+    for g in range(4):
+
+        def done(v, g=g):
+            for k in range(3):
+                gq_ref[:, k * 512 + g * 128 : k * 512 + g * 128 + 128] = v[:, k * 128 : k * 128 + 128]
+
+        pieces.append(
+            (qgrad.at[g], 0, 384, g % 2 == 0, None, sq.at[g], r1q.at[g], r2q.at[g], r3q.at[g], r4q.at[g], done)
+        )
+    sca = Scatter(me, pieces, ssem, rsem)
+    bh = remote(br_ref.at[:, 0:16, :], bhalo, hss.at[0], hrs.at[0], me.over_y)
+    bh.start()
+    for k in range(4):
+        sca.start(k, 0)
+    load_c = local(ctxt_h, ctxt, 0)
+    load_p = local(wp_h, wp, 1)
+    load_q = local(qkv_save.at[0], qb, 2)
+    load_a = local(att_save, a_ref, 3)
+    load_n = local(normt_h, normt, 4)
+    load_t = local(nt_h, nt, 5)
+    load_w = local(wqb_h, wq, 6)
+    load_m = local(mg_h, mg, 7)
+    for b in range(8):
+        for k in range(4):
+            bs[k, b * 256 : b * 256 + 240, :] = br_ref[b, 16:256, k * 128 : k * 128 + 128].astype(F32)
+    bh.wait_recv()
+    for b in range(8):
+        for k in range(4):
+            bs[k, b * 256 + 240 : b * 256 + 256, :] = bhalo[b, :, k * 128 : k * 128 + 128].astype(F32)
+    for p in range(16):
+        lo, hi = spots(p)
+        for k in range(4):
+            bp[p * 128 : p * 128 + 128, k * 128 : k * 128 + 128] = gathered(bs.at[k], lo, hi).astype(BF)
+    sca.advance(0, 0)
+    sca.advance(1, 0)
+    load_c.wait()
+    pgrad[...] = dot(ctxt[...], bp[...]).astype(BF).reshape(4, 2, 2, 2, 16, 512)
+    sca.start(4, 0)
+    sca.start(5, 0)
+    load_p.wait()
+    load_a.wait()
+    cells[...] = jnp.zeros_like(cells)
+    plan = [
+        [(2, 0), (3, 0)],
+        [(0, 1), (1, 1)],
+        [(4, 0), (5, 0)],
+        [(2, 1), (3, 1)],
+        [(0, 2), (1, 2)],
+        [(6, 0), (4, 1), (5, 1)],
+        [(2, 2), (3, 2)],
+        [(0, 3), (1, 3)],
+        [(6, 1), (7, 0), (4, 2), (5, 2)],
+        [(6, 2), (7, 1)],
+        [(2, 3), (3, 3), (4, 3), (5, 3)],
+        [(6, 3), (7, 2), (8, 0)],
+        [(8, 1), (7, 3)],
+        [(9, 0)],
+        [(8, 2), (9, 1)],
+        [(8, 3), (9, 2)],
+        [(9, 3)],
+    ]
+
+    def progress():
+        if plan:
+            for k, s in plan.pop(0):
+                sca.advance(k, s)
+
+    lanes = lax.broadcasted_iota(jnp.int32, (16, 128), 1)
+    for g in range(4):
+        fs = slice(g * 128, (g + 1) * 128)
+
+        def context_grad(t, carry, fs=fs):
+            out = dot(wp[fs, :], bp[pl.ds(pl.multiple_of(t * 512, 512), 512), :], NT)
+            for k in range(4):
+                dc[pl.ds(t * 4 + k, 128, stride=16), :] = (
+                    out[:, k * 128 : (k + 1) * 128].astype(BF).astype(F32)
+                )
+            return carry
+
+        lax.fori_loop(0, 4, context_grad, 0)
+        load_q.wait()
+
+        def widen(i, carry):
+            rows = pl.ds(pl.multiple_of(i * 512, 512), 512)
+            g_ref[rows, :] = qb[rows, :].astype(F32)
+            return carry
+
+        lax.fori_loop(0, 12, widen, 0)
+        if g < 3:
+            load_q = local(qkv_save.at[g + 1], qb, 2)
+        progress()
+
+        def head(h, carry, g=g):
+            da = pair_products(dc, h * 32, g_ref, 256 + h * 32)
+            a0 = (g * 4 + h) * 16
+            at = [tile(a_ref, a0 + q) for q in range(16)]
+            tot = tree([da[q] * at[q] for q in range(16)])
+            ds = []
+            mine = lanes == g * 4 + h
+            for q in range(16):
+                low_ref[q * 16 : q * 16 + 16, :] = at[q].astype(BF).astype(F32)
+                d = (at[q] * (da[q] - tot)).astype(BF).astype(F32)
+                ds_ref[q * 16 : q * 16 + 16, :] = d
+                ds.append(d)
+                cell = jnp.sum(d, axis=1, keepdims=True)
+                cells[q * 16 : q * 16 + 16, :] += jnp.where(mine, cell, 0.0)
+            weighted(ds, g_ref, 128 + h * 32, dg, h * 32, SCALE)
+            turned = [ds_ref[pl.ds(p, 16, stride=16), :] for p in range(16)]
+            weighted(turned, g_ref, h * 32, dg, 128 + h * 32, SCALE)
+            turned = [low_ref[pl.ds(p, 16, stride=16), :] for p in range(16)]
+            weighted(turned, dc, h * 32, dg, 256 + h * 32, None)
+            return carry
+
+        lax.fori_loop(0, 2, head, 0)
+        progress()
+        lax.fori_loop(2, 4, head, 0)
+        sums = jnp.zeros((384, 128), F32)
+        for p in range(16):
+            v = dg[pl.ds(p, 384, stride=16), :]
+            sums = sums + v
+            dqt[g * 384 : (g + 1) * 384, p * 128 : (p + 1) * 128] = v.astype(BF)
+        ar[g, 2:3, :] = jnp.sum(sums[0:128].T, 0, keepdims=True)
+        ar[g, 3:4, :] = jnp.sum(sums[256:384].T, 0, keepdims=True)
+        if g == 0:
+            load_n.wait()
+        for k in range(3):
+            rows = slice(g * 384 + k * 128, g * 384 + k * 128 + 128)
+            qgrad[g, :, :, :, :, :, k * 128 : k * 128 + 128] = (
+                dot(normt[...], dqt[rows, :], NT).astype(BF).reshape(4, 2, 2, 2, 16, 128)
+            )
+        sca.start(6 + g, 0)
+        progress()
+    load_w.wait()
+    load_t.wait()
+    wall = wq[:, :, :, :, :, 128:1664].reshape(512, 1536)
+    gain = jnp.broadcast_to(wq_gain(wq), (512, 128))
+    gacc[...] = jnp.zeros_like(gacc)
+
+    def norm_back(t, carry):
+        e4 = dot(wall, dqt[:, pl.ds(pl.multiple_of(t * 512, 512), 512)])
+        for k in range(4):
+            p = t * 4 + k
+            e = e4[:, k * 128 : (k + 1) * 128]
+            n = nt[:, pl.ds(pl.multiple_of(p * 128, 128), 128)].astype(F32)
+            gacc[0] += e * n
+            gacc[1] += e
+            eg = e * gain
+            m2 = jnp.mean(eg * n, 0, keepdims=True)
+            r = (eg - jnp.mean(eg, 0, keepdims=True) - n * m2) * rs_ref[pl.ds(p, 1), :]
+            lo = t * 8 + (k + 2) % 8
+            hi = t * 8 + (k + 6) % 8
+            for q in range(4):
+                turned = r[q * 128 : q * 128 + 128].T
+                bs[q, pl.ds(lo, 64, stride=32), :] = turned[0:64]
+                bs[q, pl.ds(hi, 64, stride=32), :] = turned[64:128]
+        return carry
+
+    for t in range(4):
+        lax.fori_loop(t, t + 1, norm_back, 0)
+        progress()
+    for b in range(8):
+        for k in range(4):
+            rout[b, :, k * 128 : k * 128 + 128] = bs[k, b * 256 + 240 : b * 256 + 256, :].astype(BF)
+    rh = remote(rout, rhalo, hss.at[1], hrs.at[1], me.over_y)
+    rh.start()
+    for zz in range(4):
+        ls = slice(zz * 128, zz * 128 + 128)
+        for k in range(2):
+            ar[zz, k : k + 1, :] = jnp.sum(gacc[k, ls, :].T, 0, keepdims=True)
+        ar[zz, 4:8, :] = small_ref[4:8, ls]
+        for k in range(4):
+            ar[zz, 8 + k : 9 + k, :] = small_ref[8 + zz : 9 + zz, k * 128 : k * 128 + 128]
+        ar[zz, 12:16, :] = jnp.zeros((4, 128), F32)
+    pair = lax.broadcasted_iota(jnp.int32, (64, 256), 1)
+    entry = lax.broadcasted_iota(jnp.int32, (64, 256), 0)
+    qi, pi = pair // 16, pair % 16
+    index = (pi // 4 - qi // 4 + 3) * 7 + pi % 4 - qi % 4 + 3
+    table = lax.dot_general(
+        (index == entry).astype(F32), cells[...], (((1,), (0,)), ((), ())),
+        precision=lax.Precision.HIGHEST, preferred_element_type=F32,
+    )
+    packed = table[0:8]
+    for k in range(1, 8):
+        packed = packed + pltpu.roll(table[8 * k : 8 * k + 8], 16 * k, 1)
+    ar[4, 0:8, :] = packed
+    ar[4, 8:16, :] = jnp.zeros((8, 128), F32)
+    progress()
+    small = [
+        remote(ar, arr.at[0], asems.at[0], aremr.at[0], me.over_core),
+        remote(ar, arr.at[1], asems.at[1], aremr.at[1], me.over_x),
+        remote(ar, arr.at[2], asems.at[2], aremr.at[2], me.over_y),
+    ]
+    small[0].start()
+    load_m.wait()
+
+    def finish(half):
+        for b in range(half * 4, half * 4 + 4):
+            for k in range(4):
+                ls = slice(k * 128, k * 128 + 128)
+                ig_ref[b, 16:256, ls] = (mg[b, 16:256, ls] + bs[k, b * 256 : b * 256 + 240, :]).astype(BF)
+
+    finish(0)
+    small[0].wait()
+    ar[...] = ar[...] + arr[0]
+    small[1].start()
+    progress()
+    finish(1)
+    small[1].wait()
+    ar[...] = ar[...] + arr[1]
+    small[2].start()
+    progress()
+    rh.wait()
+    for b in range(8):
+        ig_ref[b, 0:16, :] = (mg[b, 0:16, :] + rhalo[b].astype(F32)).astype(BF)
+    small[2].wait()
+    ar[...] = ar[...] + arr[2]
+    last = []
+    for d in range(3):
+        to = (z + 1 + d) % 4
+        last.append(remote(ar.at[to], arz.at[z, 0], asems.at[3 + d], aremr.at[3 + d], me.along_z[d]))
+        last.append(remote(ar.at[4], arz.at[z, 1], asems.at[6 + d], aremr.at[6 + d], me.along_z[d]))
+    for cp in last:
+        cp.start()
+    arz[z, 0] = ar[z]
+    arz[z, 1] = ar[4]
+    while plan:
+        progress()
+    for cp in last:
+        cp.wait()
+    total = (arz[0] + arz[1]) + (arz[2] + arz[3])
+    tab_ref[...] = total[1, 0:8]
+    ar[0] = total[0]
+    mine = pltpu.roll(total[0], (8 - me.rank8) * 16 % 128, 1)
+    for k, ref in enumerate((v0, v1, v2, v3, v4, v5, v6, v7)):
+        ref[...] = mine[k : k + 1, 0:16]
+    fb = ar[0, pl.ds(8 + x * 2 + c, 1), :]
+    fb_ref[...] = jnp.where(y == 0, fb[:, 0:64], fb[:, 64:128])
+    bh.wait_send()
+    sca.close()
+
+
+def wq_gain(wq):
+    parts = []
+    for zz in range(4):
+        total = jnp.sum(wq[zz, :, :, :, :, 0:128].astype(F32).reshape(8, 16, 128), axis=0)
+        parts.append(total.T[:, 0:1])
+    return jnp.concatenate(parts, 0)
+
+
+def k3_call(br, mg, g1, g2, small, wqb, wp, qs, asv, ctxt, normt, nt, rs):
+    S = jax.ShapeDtypeStruct
+    V = pltpu.VMEM
+    lead = (4, 2, 2, 2)
+    half = (4, 2, 2)
+    outs = [S((8, 256, 512), BF), S((16, 1536), F32), S((16, 512), F32), S((16, 2048), F32), S((64, 512), F32)]
+    outs += [S((1, 16), F32)] * 8 + [S((1, 64), F32), S((8, 128), F32)]
+
+    def four(shape):
+        return [V(shape + (64, 256), BF)] * 2 + [V(shape + (16, 1024), BF)] * 2
+
+    fours = [four(half), four(half), four((4, 2)), four((4,)), four((3,))]
+    rest = []
+    for count, n in ((2, 256), (4, 384)):
+        for shape in (half, half, (4, 2), (4,), (3,)):
+            rest.append(V((count,) + shape + (16, n), BF))
+    scratch = [
+        V((4, 2048, 128), F32), V((2048, 512), BF), V((8, 256, 512), F32), V(lead + (16, 1664), BF),
+        V((512, 512), BF), V((6144, 128), BF), V((6144, 128), F32), V((6144, 128), F32),
+        V((2048, 128), F32), V((4096, 128), F32), V((1536, 2048), BF), V((512, 2048), BF),
+        V((512, 2048), BF), V((512, 2048), BF), V((256, 128), F32), V((256, 128), F32),
+        V((2, 512, 128), F32), V(lead + (16, 512), BF), V((4,) + lead + (16, 384), BF),
+        V((8, 16, 512), BF), V((8, 16, 512), BF), V((8, 16, 512), BF), V((256, 128), F32),
+        V((5, 16, 128), F32), V((3, 5, 16, 128), F32), V((4, 2, 16, 128), F32),
+    ]
+    sems = [
+        pltpu.SemaphoreType.DMA((10, 6)), pltpu.SemaphoreType.DMA((10, 6)),
+        pltpu.SemaphoreType.DMA((2,)), pltpu.SemaphoreType.DMA((2,)), pltpu.SemaphoreType.DMA((14,)),
+        pltpu.SemaphoreType.DMA((9,)), pltpu.SemaphoreType.DMA((9,)),
+    ]
+
+    def body(*refs):
+        n = 13 + len(outs) + len(scratch)
+        flat = refs[n : n + 20]
+        groups = [flat[i * 4 : i * 4 + 4] for i in range(5)]
+        k3_body(*refs[:n], *groups, *refs[n + 20 :])
+
+    return pl.pallas_call(
+        body,
+        out_shape=outs,
+        in_specs=[VM, HB, HB, HB, VM, HB, HB, HB, HB, HB, HB, HB, VM],
+        out_specs=[VM] * len(outs),
+        scratch_shapes=scratch + sum(fours, []) + rest + sems,
+        compiler_params=pltpu.CompilerParams(
+            collective_id=2, has_side_effects=True, vmem_limit_bytes=62 << 20
+        ),
+        name="attend_back_scatter",
+    )(br, mg, g1, g2, small, wqb, wp, qs, asv, ctxt, normt, nt, rs)
 
 
 HEADS = 16
@@ -712,192 +1224,26 @@
         v.reshape(1, 16)
         for v in (ln1_gain, ln1_bias, q_bias, v_bias, proj_bias, ln2_gain, ln2_bias, fc2_bias)
     ]
+    shape = inputs.shape
+    x = inputs.reshape(8, 256, 512)
     ctx, wqb, wpb, w1b, w2b, par, qs, asv, ctxt, normt, nt, rs = k1_call(
-        inputs.reshape(8, 256, 512), w_qkv, w_proj, w_fc1, w_fc2, smalls, fc1_bias.reshape(1, 64), bt
-    )
-    gain_one, bias_one, qbias_full, vbias_full, pbias_full, gain_two, bias_two, fc2b_full = (
-        par[i] for i in range(8)
-    )
-    fc1b_full = par[8:12].reshape(2048)
-    qkv_full = (
-        wqb.reshape(512, 1664)[:, 128:].reshape(512, 4, 3, 128).transpose(0, 2, 1, 3).reshape(512, 1536)
-    )
-    proj_full, fc1_full, fc2_full = wpb.reshape(512, 512), w1b.reshape(512, 2048), w2b.reshape(2048, 512)
-    clip_count, row_count, column_count, feature_width = inputs.shape
-    score_scale = 1.0 / math.sqrt(HEAD_DIM)
-    float_type = jnp.float32
-    half_type = jnp.bfloat16
-    ahead = from_behind(inputs[:, :SHIFT], "slab", -1)
-    window_rows = jnp.concatenate([inputs[:, SHIFT:], ahead], axis=1).astype(float_type)
-    normed, first_pull = jax.vjp(
-        normalize, window_rows, gain_one.astype(float_type), bias_one.astype(float_type)
-    )
-    windows = to_windows(jnp.roll(normed.astype(half_type), -SHIFT, axis=2))
-    window_count = windows.shape[0]
-    token_count = window_count * WIN * WIN
-    head_shape = (window_count, WIN * WIN, HEADS, HEAD_DIM)
-    flat_windows = windows.reshape(token_count, feature_width)
-    projected = jnp.dot(flat_windows, qkv_full, preferred_element_type=float_type)
-    query_heads = (
-        (projected[:, :feature_width] + qbias_full.astype(float_type))
-        .astype(half_type)
-        .reshape(head_shape)
-    )
-    key_heads = (
-        projected[:, feature_width : 2 * feature_width].astype(half_type).reshape(head_shape)
-    )
-    value_heads = (
-        (projected[:, 2 * feature_width :] + vbias_full.astype(float_type))
-        .astype(half_type)
-        .reshape(head_shape)
-    )
-    onehot = table_onehot()
-    position_bias = (
-        jnp.dot(onehot, pos_table, precision=highest)
-        .reshape(WIN * WIN, WIN * WIN, HEADS)
-        .transpose(2, 0, 1)
-    )
-    scores = (
-        jnp.einsum("wqhc,wkhc->whqk", query_heads, key_heads, preferred_element_type=float_type)
-        * score_scale
-        + position_bias[None]
-    )
-    attention = jax.nn.softmax(scores, axis=-1)
-    attention_low = attention.astype(half_type)
-    context = jnp.einsum(
-        "whqk,wkhc->wqhc", attention_low, value_heads, preferred_element_type=float_type
-    )
-    context = context.astype(half_type).reshape(window_count, WIN * WIN, feature_width)
-    context_grid = jnp.roll(
-        from_windows(context, clip_count, row_count, column_count), SHIFT, axis=2
-    )
-    returned = from_behind(context_grid[:, row_count - SHIFT :], "slab", 1)
-    own_flat = jnp.concatenate([returned, context_grid[:, : row_count - SHIFT]], axis=1).reshape(
-        -1, feature_width
-    )
-    own_flat = ctx.reshape(-1, feature_width)
-    input_flat = inputs.reshape(-1, feature_width).astype(float_type)
-    middle = (
-        input_flat
-        + jnp.dot(own_flat, proj_full, preferred_element_type=float_type)
-        + pbias_full.astype(float_type)
-    )
-    second, second_pull = jax.vjp(
-        normalize, middle, gain_two.astype(float_type), bias_two.astype(float_type)
-    )
-    second_low = second.astype(half_type)
-    pre_act = jnp.dot(second_low, fc1_full, preferred_element_type=float_type) + fc1b_full.astype(
-        float_type
-    )
-    hidden, gelu_pull = jax.vjp(exact_gelu, pre_act)
-    hidden_low = hidden.astype(half_type)
-    output = (
-        middle
-        + jnp.dot(hidden_low, fc2_full, preferred_element_type=float_type)
-        + fc2b_full.astype(float_type)
-    )
-    incoming = (cotangent.astype(float_type) * grad_mask.astype(float_type)[..., None]).reshape(
-        -1, feature_width
-    )
-    incoming_low = incoming.astype(half_type)
-    fc2_grad = outer_sum(hidden_low, incoming_low)
-    fc2b_grad = jnp.sum(incoming, axis=0)
-    hidden_grad = times_transposed(incoming_low, fc2_full)
-    pre_grad = gelu_pull(hidden_grad)[0].astype(half_type)
-    fc1_grad = outer_sum(second_low, pre_grad)
-    fc1b_grad = jnp.sum(pre_grad.astype(float_type), axis=0)
-    second_grad = times_transposed(pre_grad, fc1_full)
-    middle_part, gain_two_grad, bias_two_grad = second_pull(second_grad)
-    middle_grad = incoming + middle_part
-    branch_low = middle_grad.astype(half_type)
-    proj_grad = outer_sum(own_flat, branch_low)
-    pbias_grad = jnp.sum(branch_low.astype(float_type), axis=0)
-    context_grad = (
-        times_transposed(branch_low, proj_full)
-        .astype(half_type)
-        .reshape(clip_count, row_count, column_count, feature_width)
-    )
-    sent_back = from_behind(context_grad[:, :SHIFT], "slab", -1)
-    window_context_grad = jnp.concatenate([context_grad[:, SHIFT:], sent_back], axis=1)
-    context_heads = to_windows(jnp.roll(window_context_grad, -SHIFT, axis=2)).reshape(head_shape)
-    value_grad = jnp.einsum(
-        "whqk,wqhc->wkhc", attention_low, context_heads, preferred_element_type=float_type
-    ).astype(half_type)
-    attention_grad = jnp.einsum(
-        "wqhc,wkhc->whqk", context_heads, value_heads, preferred_element_type=float_type
-    )
-    score_grad = (
-        attention * (attention_grad - jnp.sum(attention_grad * attention, -1, keepdims=True))
-    ).astype(half_type)
-    bias_cells = (
-        jnp.sum(score_grad.astype(float_type), axis=0)
-        .transpose(1, 2, 0)
-        .reshape(WIN * WIN * WIN * WIN, HEADS)
-    )
-    table_grad = lax.dot_general(onehot, bias_cells, (((0,), (0,)), ((), ())), precision=highest)
-    query_grad = (
-        jnp.einsum("whqk,wkhc->wqhc", score_grad, key_heads, preferred_element_type=float_type)
-        * score_scale
-    ).astype(half_type)
-    key_grad = (
-        jnp.einsum("whqk,wqhc->wkhc", score_grad, query_heads, preferred_element_type=float_type)
-        * score_scale
-    ).astype(half_type)
-    query_flat = query_grad.reshape(token_count, feature_width)
-    value_flat = value_grad.reshape(token_count, feature_width)
-    qkv_grad_low = jnp.concatenate(
-        [query_flat, key_grad.reshape(token_count, feature_width), value_flat], axis=1
-    )
-    qkv_grad = outer_sum(flat_windows, qkv_grad_low)
-    qbias_grad = jnp.sum(query_flat.astype(float_type), axis=0)
-    vbias_grad = jnp.sum(value_flat.astype(float_type), axis=0)
-    normed_grad = times_transposed(qkv_grad_low, qkv_full).reshape(
-        window_count, WIN * WIN, feature_width
-    )
-    normed_grid_grad = jnp.roll(
-        from_windows(normed_grad, clip_count, row_count, column_count), SHIFT, axis=2
-    )
-    rows_part, gain_one_grad, bias_one_grad = first_pull(normed_grid_grad)
-    halo_back = from_behind(
-        rows_part[:, row_count - SHIFT :].astype(jnp.bfloat16), "slab", 1
-    ).astype(jnp.float32)
-    input_grad = middle_grad.reshape(
-        clip_count, row_count, column_count, feature_width
-    ) + jnp.concatenate([halo_back, rows_part[:, : row_count - SHIFT]], axis=1)
-    shares = (
-        lax.psum_scatter(gain_one_grad, ("clip", "slab"), scatter_dimension=0, tiled=True),
-        lax.psum_scatter(bias_one_grad, ("clip", "slab"), scatter_dimension=0, tiled=True),
-        lax.psum_scatter(qkv_grad, ("clip", "slab"), scatter_dimension=0, tiled=True),
-        lax.psum_scatter(qbias_grad, ("clip", "slab"), scatter_dimension=0, tiled=True),
-        lax.psum_scatter(vbias_grad, ("clip", "slab"), scatter_dimension=0, tiled=True),
-        lax.psum_scatter(proj_grad, ("clip", "slab"), scatter_dimension=0, tiled=True),
-        lax.psum_scatter(pbias_grad, ("clip", "slab"), scatter_dimension=0, tiled=True),
-        lax.psum_scatter(gain_two_grad, ("clip", "slab"), scatter_dimension=0, tiled=True),
-        lax.psum_scatter(bias_two_grad, ("clip", "slab"), scatter_dimension=0, tiled=True),
-        lax.psum_scatter(fc1_grad, ("clip", "slab"), scatter_dimension=0, tiled=True),
-        lax.psum_scatter(fc1b_grad, ("clip", "slab"), scatter_dimension=0, tiled=True),
-        lax.psum_scatter(fc2_grad, ("clip", "slab"), scatter_dimension=0, tiled=True),
-        lax.psum_scatter(fc2b_grad, ("clip", "slab"), scatter_dimension=0, tiled=True),
-    )
-    table_total = lax.psum(table_grad, ("clip", "slab"))
-    output = output.reshape(clip_count, row_count, column_count, feature_width).astype(half_type)
+        x, w_qkv, w_proj, w_fc1, w_fc2, smalls, fc1_bias.reshape(1, 64), bt
+    )
+    wp = wpb.reshape(512, 512)
+    output, mg, br, g1, g2, small = k2_call(
+        x.reshape(2048, 512), ctx.reshape(2048, 512), cotangent.reshape(2048, 512), grad_mask, par,
+        wp, w1b.reshape(512, 2048), w2b.reshape(2048, 512)
+    )
+    lead = (4, 2, 2, 2)
+    input_grad, gq, gp, gf1, gf2, *vectors, fb, tab = k3_call(
+        br.reshape(8, 256, 512), mg.reshape(8, 256, 512), g1.reshape(lead + (16, 2048)),
+        g2.reshape(lead + (64, 512)), small, wqb, wp, qs, asv, ctxt, normt, nt, rs
+    )
+    v = [r.reshape(16) for r in vectors]
+    table = tab.reshape(8, 8, 16).transpose(1, 0, 2).reshape(64, 16)[:TABLE]
     return (
-        output,
-        input_grad.astype(half_type),
-        shares[0],
-        shares[1],
-        shares[2],
-        shares[3],
-        shares[4],
-        shares[5],
-        shares[6],
-        shares[7],
-        shares[8],
-        shares[9],
-        shares[10],
-        shares[11],
-        shares[12],
-        table_total,
+        output.reshape(shape), input_grad.reshape(shape), v[0], v[1], gq, v[2], v[3], gp, v[4], v[5],
+        v[6], gf1, fb.reshape(64), gf2, v[7], table,
     )
 
 

time: 851 us -> 238 us (0.28)
  waiting for transfers between devices: 235 us -> 0 us
  matrix products: 205 us -> 0.2 us
  local copies, waits for them, and re-layouts: 197 us -> 14.7 us
  Pallas kernels: 69.4 us -> 218 us
  other arithmetic: 75.2 us -> 0.08 us
  blocking collectives: 41.6 us -> 0 us
  between operations: 14.9 us -> 1.05 us
    reduce_scatter x4 -> x0, waiting for transfers between devices: 235 us -> none  [the longest x1 141 us: per_device_fast(): lax.psum_scatter(fc2_grad, ('clip', 'slab'), scatter_dimension=0, tiled=T...]
    dot_general x18 -> x0, matrix products: 205 us -> none  [the longest x1 43.7 us: per_device_fast(): jnp.dot(second_low, fc1_full, preferred_element_type=float_type)]
    pallas_call x0 -> x2, Pallas kernels: none -> 147 us  [the longest x1 91.3 us: k3_call(): pl.pallas_call(body, out_shape=outs, in_specs=[VM, HB, HB, HB, VM, HB, HB...]
    reshape x10 -> x2, local copies, waits for them, and re-layouts: 67.2 us -> 0.76 us  [per_device_fast(): table = tab.reshape(8, 8, 16).transpose(1, 0, 2).reshape(64, 16)[:TABLE]]
    concatenate x7 -> x0, local copies, waits for them, and re-layouts: 42.3 us -> none  [the longest x6 41.4 us: per_device_fast(): jnp.concatenate([query_flat, key_grad.reshape(token_count, feature_width)...]
    unnamed x1 -> x0, blocking collectives: 41.6 us -> none
    convert_element_type x4 -> x0, local copies, waits for them, and re-layouts: 32.6 us -> none  [the longest x1 10.8 us: per_device_fast(): key_grad = (jnp.einsum('whqk,wqhc->wkhc', score_grad, query_heads, prefer...]
    reduce_sum x12 -> x0, other arithmetic: 32 us -> none  [the longest x1 15.4 us: per_device_fast(): jnp.sum(score_grad.astype(float_type), axis=0).transpose(1, 2, 0)]
  transfers between devices with their start and end apart: 7 -> 0, of which waited for: 2 -> 0; matrix products, arithmetic and copies ran while one was open for 55% -> 0% of each run, Pallas kernels for 8% -> 0%
where the time goes in v2:
time: 238 us; the launch traced here: 234 us
  Pallas kernels  218 us (92%)
  local copies, waits for them, and re-layouts  14.7 us (6%)
    pallas_call x1, Pallas kernels, k3_call(): pl.pallas_call(body, out_shape=outs, in_specs=[VM, HB, HB, HB, VM, HB, HB...  91.3 us
    pallas_call x1, Pallas kernels, k1_call(): pl.pallas_call(k1_body, out_shape=[o[0] for o in outs], in_specs=[VM, VM,...  70.5 us
    pallas_call x1, Pallas kernels, k2_call(): pl.pallas_call(k2_body, out_shape=[S((2048, 512), BF), S((2048, 512), F32...  55.9 us
    unnamed x44, local copies, waits for them, and re-layouts  13.1 us

profile of v2, /device:TPU:0, one launch (start us, length us, event | category | flops | bytes accessed | tf_op | source)
XLA Modules:
  0.0 233.8 jit_solution(1167314196841395570)
XLA Ops:
  0.6 0.0 copy-start
  0.7 0.1 subtract_add_fusion
  0.7 0.1 reshape.246
  0.8 0.5 copy-done
  1.3 0.2 fusion
  1.5 0.8 reshape.221
  2.4 1.5 copy.35.mask_ref
  3.9 70.5 %gather_attend.1 = (bf16[8,256,512]{2,1,0:T(8,128)(2,1)}, bf16[4,2,2,2,16,1664]{5,4,3,2,1,0:T(8,128)(2,1)}, bf16[4,2,2,2,16,512]{5,4,3,2,1,0:T(8,128)(2,1)}, bf1...) custom-call(bf16[8,256,512]{2,1,0:T(8,128)(2,1)} %bitcast.40, ...), custom_call_target="tpu_custom_call" | custom-call | tf_op jit(solution)/shard_map/gather_attend/pallas_call | solution.py:370
  74.4 55.9 %feed_forward.1 = (bf16[2048,512]{1,0:T(8,128)(2,1)}, f32[2048,512]{1,0:T(8,128)}, bf16[2048,512]{1,0:T(8,128)(2,1)}, bf16[512,2048]{1,0:T(8,128)(2,1)}, bf16[2048,512]{1,0:T(8,128)(2,1)}, /*index=5*/f32[16,512]{1,0:T(8,128)}) custom-call(bf16[2048,512]{1,0:T(8,128)(2,1)} %bitcast.41, bf16[2048,512]{1,0:T(8,128)(2,1)} %bitcast.50, ...), custom_call_target="tpu_custom_call" | custom-call | tf_op jit(solution)/shard_map/feed_forward/pallas_call | solution.py:483
  130.3 91.3 %attend_back_scatter.1 = (bf16[8,256,512]{2,1,0:T(8,128)(2,1)}, f32[16,1536]{1,0:T(8,128)}, f32[16,512]{1,0:T(8,128)}, f32[16,2048]{1,0:T(8,128)}, f32[64,512]{1...) custom-call(bf16[8,256,512]{2,1,0:T(8,128)(2,1)} %bitcast.43, ...), custom_call_target="tpu_custom_call" | custom-call | tf_op jit(solution)/shard_map/attend_back_scatter/pallas_call | solution.py:889
  221.6 0.8 reshape.242
  222.4 0.7 copy.37
  223.1 0.0 copy-start.10
  223.1 0.0 copy-start.4
  223.1 0.0 copy-start.9
  223.1 0.0 copy-start.8
  223.1 0.0 copy-start.7
  223.1 0.0 copy-start.2
  223.1 0.0 copy-start.6
  223.1 0.0 copy-start.1
  223.1 0.0 copy-start.5
  223.2 3.1 %copy.54 = bf16[8,32,8,512]{3,2,1,0:T(8,128)(2,1)} copy(bf16[8,32,8,512]{3,2,1,0:T(8,128)(2,1)} %bitcast.48) | data formatting | bytes 4194304
  226.3 0.0 copy-done.13
  226.3 0.5 copy.55
  226.8 0.0 copy-done.12
  226.8 0.5 copy.56
  227.3 0.0 copy-done.3
  227.3 0.6 copy.57
  228.0 0.0 copy-done.11
  228.0 0.5 copy.58
  228.5 0.0 copy-done.10
  228.5 0.5 copy.59
  229.0 0.0 copy-done.4
  229.0 0.6 copy.60
  229.6 0.0 copy-done.9
  229.6 0.5 copy.61
  230.1 0.0 copy-done.8
  230.1 0.5 copy.62
  230.6 0.0 copy-done.7
  230.6 0.5 copy.63
  231.2 0.0 copy-done.2
  231.2 0.7 copy.64
  231.8 0.0 copy-done.6
  231.8 0.5 copy.65
  232.3 0.0 copy-done.1
  232.3 0.7 copy.66
  233.0 0.0 copy-done.5
  233.0 0.5 copy.67
  (7 shorter events, 0.0 us)
Async XLA Ops:
  0.6 0.7 copy-start
  223.1 3.2 %copy-start.13 = (f32[1,16]{1,0:T(1,128)S(1)}, f32[1,16]{1,0:T(1,128)}, u32[]{:S(2)}) copy-start(f32[1,16]{1,0:T(1,128)} %get-tuple-element.68) | copy-start | bytes 196
  223.1 3.7 %copy-start.12 = (f32[1,16]{1,0:T(1,128)S(1)}, f32[1,16]{1,0:T(1,128)}, u32[]{:S(2)}) copy-start(f32[1,16]{1,0:T(1,128)} %get-tuple-element.69) | copy-start | bytes 196
  223.1 4.3 %copy-start.3 = (f32[16,1536]{1,0:T(8,128)S(1)}, f32[16,1536]{1,0:T(8,128)}, u32[]{:S(2)}) copy-start(f32[16,1536]{1,0:T(8,128)} %get-tuple-element.120) | copy-start | bytes 294916
  223.1 4.9 %copy-start.11 = (f32[1,16]{1,0:T(1,128)S(1)}, f32[1,16]{1,0:T(1,128)}, u32[]{:S(2)}) copy-start(f32[1,16]{1,0:T(1,128)} %get-tuple-element.71) | copy-start | bytes 196
  223.1 5.4 %copy-start.10 = (f32[1,16]{1,0:T(1,128)S(1)}, f32[1,16]{1,0:T(1,128)}, u32[]{:S(2)}) copy-start(f32[1,16]{1,0:T(1,128)} %get-tuple-element.72) | copy-start | bytes 196
  223.1 5.9 %copy-start.4 = (f32[16,512]{1,0:T(8,128)S(1)}, f32[16,512]{1,0:T(8,128)}, u32[]{:S(2)}) copy-start(f32[16,512]{1,0:T(8,128)} %get-tuple-element.123) | copy-start | bytes 98308
  223.1 6.5 %copy-start.9 = (f32[1,16]{1,0:T(1,128)S(1)}, f32[1,16]{1,0:T(1,128)}, u32[]{:S(2)}) copy-start(f32[1,16]{1,0:T(1,128)} %get-tuple-element.74) | copy-start | bytes 196
  223.1 7.0 %copy-start.8 = (f32[1,16]{1,0:T(1,128)S(1)}, f32[1,16]{1,0:T(1,128)}, u32[]{:S(2)}) copy-start(f32[1,16]{1,0:T(1,128)} %get-tuple-element.75) | copy-start | bytes 196
  223.1 7.5 %copy-start.7 = (f32[1,16]{1,0:T(1,128)S(1)}, f32[1,16]{1,0:T(1,128)}, u32[]{:S(2)}) copy-start(f32[1,16]{1,0:T(1,128)} %get-tuple-element.76) | copy-start | bytes 196
  223.1 8.0 %copy-start.2 = (f32[16,2048]{1,0:T(8,128)S(1)}, f32[16,2048]{1,0:T(8,128)}, u32[]{:S(2)}) copy-start(f32[16,2048]{1,0:T(8,128)} %get-tuple-element.127) | copy-start | bytes 393220
  223.1 8.7 %copy-start.6 = (f32[1,64]{1,0:T(1,128)S(1)}, f32[1,64]{1,0:T(1,128)}, u32[]{:S(2)}) copy-start(f32[1,64]{1,0:T(1,128)} %get-tuple-element.78) | copy-start | bytes 772
  223.1 9.2 %copy-start.1 = (f32[64,512]{1,0:T(8,128)S(1)}, f32[64,512]{1,0:T(8,128)}, u32[]{:S(2)}) copy-start(f32[64,512]{1,0:T(8,128)} %get-tuple-element.129) | copy-start | bytes 393220
  223.1 9.8 %copy-start.5 = (f32[1,16]{1,0:T(1,128)S(1)}, f32[1,16]{1,0:T(1,128)}, u32[]{:S(2)}) copy-start(f32[1,16]{1,0:T(1,128)} %get-tuple-element.80) | copy-start | bytes 196
